TPU v7x, 512 devices: a whole 4x8x8 slice. The times are simulated.
512 devices in a mesh: dp: 16 (over y, core), proj: 32 (over x, z).
Axes of the slice: x: 4, y: 8, z: 8, core: 2. Of those that a mesh axis runs over, the one named last changes fastest.
Arguments:
- cotangents: bfloat16 [2048, 64, 8192], P(('dp', 'proj')), may hold values from -6 to 6
- adapter_activations: bfloat16 [2048, 64, 128], P(('dp', 'proj')), may hold values from -6 to 6
- lengths: int32 [2048], P(('dp', 'proj')), may hold values from 16 to 64
- column_factors: bfloat16 [4, 8192, 256], P(None, 'proj'), may hold values from -1 to 1, as said below
- row_factors: bfloat16 [4, 32, 32], replicated, may hold values from -1 to 1, as said below
- targets: bfloat16 [256, 8192], P('dp', 'proj'), may hold values from -16 to 16
Outputs:
- scores: float32 [2048, 256], P('dp')
Inputs may be any that keep to these rules, and one draw needn't show every extreme that they name: `column_factors`: every entry is +1 or -1. `row_factors`: every entry is +1 or -1.
All inputs are finite; a program needn't handle non-finite values.
Results may differ from a plain program's by a relative error of at most 0.0029.
Values may be sent and summed in bfloat16 or wider, within the bound.
A program may use at most 128 MiB of HBM per device.

v0:
```python
import math

import jax
import jax.numpy as jnp
from jax import lax
from jax.sharding import PartitionSpec as P

FEATURE_DIM = 8192


epsilon = 1e-06


def masked_activations(adapter_activations, lengths):
    token_positions = lax.broadcasted_iota(jnp.int32, adapter_activations.shape[:2], 1)
    token_valid_mask = (token_positions < lengths[:, None]).astype(jnp.bfloat16)
    return adapter_activations * token_valid_mask[:, :, None]


def on_device(cotangents, adapter_activations, lengths, column_factors, row_factors, targets):
    masked_values = masked_activations(adapter_activations, lengths)
    grads = jnp.einsum(
        "etr,etd->erd", masked_values, cotangents, preferred_element_type=jnp.float32
    ).astype(jnp.bfloat16)
    owned_slices = lax.all_to_all(grads, "proj", split_axis=2, concat_axis=0, tiled=True)
    rows_all = owned_slices.shape[0]
    groups, group_rows, feature_rows = row_factors.shape
    row_f32 = row_factors.astype(jnp.float32)
    outer_terms = None
    for group in range(groups):
        rank_slab = owned_slices[:, group * group_rows : (group + 1) * group_rows, :]
        inner_terms = jnp.einsum(
            "mas,sc->mac", rank_slab, column_factors[group], preferred_element_type=jnp.float32
        )
        term = jnp.einsum(
            "ak,mac->mkc", row_f32[group], inner_terms, precision=lax.Precision.HIGHEST
        )
        outer_terms = term if outer_terms is None else outer_terms + term
    partial_value = outer_terms.reshape(rows_all, -1)
    gradient_features = lax.psum_scatter(partial_value, "proj", scatter_dimension=1, tiled=True)
    target_all = lax.all_gather(targets, "dp", axis=0, tiled=True)
    target_f32 = target_all.astype(jnp.float32)
    cand_part = jnp.sum(gradient_features * gradient_features, axis=1)
    targ_part = jnp.sum(target_f32 * target_f32, axis=1)
    cand_sq, targ_sq = lax.psum((cand_part, targ_part), "proj")
    unit_rows = gradient_features / jnp.sqrt(cand_sq + epsilon)[:, None]
    unit_targets = target_f32 / jnp.sqrt(targ_sq + epsilon)[:, None]
    dot_part = jnp.dot(unit_rows, unit_targets.T, precision=lax.Precision.HIGHEST)
    scores = math.sqrt(FEATURE_DIM) * lax.psum(dot_part, "proj")
    return scores


def solution(mesh):
    placed = (
        P(("dp", "proj"), None, None),
        P(("dp", "proj"), None, None),
        P(("dp", "proj")),
        P(None, "proj", None),
        P(),
        P("dp", "proj"),
    )
    return jax.shard_map(
        on_device, mesh=mesh, in_specs=placed, out_specs=P("dp", None), check_vma=False
    )
```

profile of v0, /device:TPU:1, one launch (start us, length us, event | category | flops | bytes accessed | tf_op | source)
XLA Modules:
  0.0 721.4 jit_solution(14372103641489044734)
XLA Ops:
  6.5 0.0 reduce-scatter.2.cloned.1.call-start
  6.5 0.7 fusion.34
  7.3 7.9 %convolution_convert_fusion = bf16[4,128,8192]{2,1,0:T(8,128)(2,1)} fusion(bf16[4,64,8192]{2,1,0:T(8,128)(2,1)} %param.6, bf16[4,64,128]{2,1,0:T(8,128)(2,1)} %param.7, bf16[4,64]{1,0:T(4,128)(2,1)S(1)} %fusion.34), kind=kOutput, calls=%fused_computation | convolution fusion | flops 541097984 | bytes 12648960 | tf_op jit(solution)/shard_map/etr,etd->erd/dot_general | solution.py:22
  15.1 13.6 %copy.21 = bf16[4,128,8192]{1,0,2:T(4,128)(2,1)} copy(bf16[4,128,8192]{2,1,0:T(8,128)(2,1)} %convolution_convert_fusion) | data formatting | bytes 16777216 | tf_op jit(solution)/shard_map/convert_element_type | solution.py:24
  28.8 195.7 %all_to_all.18 = bf16[4,128,8192]{1,0,2:T(4,128)(2,1)} all-to-all(bf16[4,128,8192]{1,0,2:T(4,128)(2,1)} %copy.21), channel_id=1, replica_groups=mesh['dp'=16,'proj'=32] {'proj'}, dimensions={2} | all-to-all | bytes 16777216 | tf_op jit(solution)/shard_map/all_to_all | solution.py:25
  224.5 7.7 %copy.22 = bf16[4,128,8192]{1,2,0:T(8,128)(2,1)} copy(bf16[4,128,8192]{1,0,2:T(4,128)(2,1)} %all_to_all.18) | data formatting | bytes 16777216 | tf_op jit(solution)/shard_map/all_to_all | solution.py:25
  232.2 0.0 copy-start.1
  232.2 12.0 %copy.23 = bf16[32,4,128,256]{3,2,1,0:T(8,128)(2,1)} copy(bf16[32,4,128,256]{2,3,0,1:T(8,128)(2,1)} %bitcast.52) | data formatting | bytes 16777216 | tf_op jit(solution)/shard_map/all_to_all | solution.py:25
  244.2 0.0 copy-done.1
  244.2 0.0 copy-start
  244.2 2.5 fusion.2
  246.7 2.9 fusion.4
  249.5 0.0 copy-done
  249.6 0.7 fusion.6
  250.3 0.0 copy-start.2
  250.3 0.7 fusion
  251.0 0.0 copy-done.2
  251.0 2.3 fusion.24
  253.4 2.3 fusion.26
  255.7 2.3 fusion.28
  258.0 3.4 add_add_fusion
  261.4 5.5 copy.32
  266.9 0.0 copy-start.3
  266.9 0.0 reduce-scatter.2.cloned.1.call-update
  266.9 0.0 all-reduce.3.cloned.1.call-start
  267.0 0.6 copy-done.3
  267.6 22.7 %all_gather.3 = bf16[256,256]{1,0:T(8,128)(2,1)S(1)} all-gather(bf16[16,256]{1,0:T(8,128)(2,1)S(1)} %copy-done.3), channel_id=1, replica_groups=mesh['dp'=16,'proj'=32] {'dp'}, dimensions={0}, use_global_device_ids=true | all-gather | bytes 139264 | tf_op jit(solution)/shard_map/all_gather | solution.py:41
  290.3 0.1 fusion.8
  290.4 200.6 %reduce-scatter.2.cloned.1.call-done = f32[128,256]{1,0:T(8,128)} async-done(((f32[128,8192]{1,0:T(8,128)}), f32[128,256]{1,0:T(8,128)}) %reduce-scatter.2.cloned.1.call-update) | async-done | bytes 131088 | tf_op jit(solution)/shard_map/reduce_scatter | solution.py:40
  491.1 1.0 multiply_reduce_fusion
  492.1 58.1 %all-reduce = (f32[256]{0:T(256)S(1)}, f32[128]{0:T(128)S(1)}) all-reduce(f32[256]{0:T(256)S(1)} %fusion.8, f32[128]{0:T(128)S(1)} %multiply_reduce_fusion), channel_id=1, replica_groups=mesh['dp'=16,'proj'=32] {'proj'}, use_global_device_ids=true, to_apply=%region_4.0 | all-reduce | flops 384 | bytes 3072 | tf_op jit(solution)/shard_map/psum | solution.py:45
  550.2 2.0 fusion.9
  552.3 0.0 all-reduce.3.cloned.1.call-update
  552.3 160.7 %all-reduce.3.cloned.1.call-done = f32[128,256]{1,0:T(8,128)} async-done(((f32[128,256]{1,0:T(8,128)}), f32[128,256]{1,0:T(8,128)}) %all-reduce.3.cloned.1.call-update) | async-done | bytes 131088 | tf_op jit(solution)/shard_map/psum | solution.py:49
  713.0 1.6 broadcast_multiply_fusion
  (2 shorter events, 0.0 us)
Async XLA Ops:
  6.5 484.5 %reduce-scatter.2.cloned.1.call-start = ((), (), s32[]{:S(2)}) async-start(), calls=%async_computation.2 | async-start | bytes 4325376 | tf_op jit(solution)/shard_map/reduce_scatter | solution.py:40
  232.2 12.0 %copy-start.1 = (bf16[4,256,256]{2,1,0:T(8,128)(2,1)S(1)}, bf16[4,256,256]{2,1,0:T(8,128)(2,1)}, u32[]{:S(2)}) copy-start(bf16[4,256,256]{2,1,0:T(8,128)(2,1)} %param.9) | copy-start | bytes 1572868
  244.2 5.3 copy-start
  250.3 0.8 copy-start.2
  266.9 0.7 copy-start.3
  266.9 446.1 %all-reduce.3.cloned.1.call-start = ((), (), s32[]{:S(2)}) async-start(), calls=%async_computation.3 | async-start | bytes 262144 | tf_op jit(solution)/shard_map/psum | solution.py:49
Sparse Core Ops, SparseCore 0:
  267.0 223.9 reduce-scatter.1
  552.4 160.5 all-reduce.2
where the time goes:
time: 726 us; the launch traced here: 721 us
  waiting for transfers between devices  361 us (50%)
  blocking collectives  277 us (38%)
  local copies, waits for them, and re-layouts  39.5 us (5%)
  matrix products  27.1 us (4%)
  between operations  13.5 us (2%)
    reduce_scatter x1, waiting for transfers between devices, on_device(): lax.psum_scatter(partial_value, 'proj', scatter_dimension=1, tiled=True)  201 us
    all_to_all x1, blocking collectives, on_device(): lax.all_to_all(grads, 'proj', split_axis=2, concat_axis=0, tiled=True)  196 us
    psum x1, waiting for transfers between devices, on_device(): scores = math.sqrt(FEATURE_DIM) * lax.psum(dot_part, 'proj')  161 us
    psum x1, blocking collectives, on_device(): cand_sq, targ_sq = lax.psum((cand_part, targ_part), 'proj')  58.1 us
    all_gather x1, blocking collectives, on_device(): target_all = lax.all_gather(targets, 'dp', axis=0, tiled=True)  22.7 us
    all_to_all x2, local copies, waits for them, and re-layouts, on_device(): lax.all_to_all(grads, 'proj', split_axis=2, concat_axis=0, tiled=True)  19.7 us
  transfers between devices with their start and end apart: 2, of which 2 were waited for; matrix products, arithmetic and copies ran while one was open for 0% of the time, Pallas kernels for 0%

commit v1 on v0

v1 whole, which is shorter than its diff:
```python
import functools
import math

import jax
import jax.numpy as jnp
from jax import lax
from jax.experimental import pallas as pl
from jax.experimental.pallas import tpu as pltpu
from jax.sharding import PartitionSpec as P

MESH = pl.DeviceIdType.MESH
EPS = 1e-06
XS, YS, ZS = 4, 8, 8
NP = XS * ZS
GR, RS, KR, KC = 4, 32, 32, 256
E, TOK, RANK = 4, 64, 128
HALF = 128
ROWS = (GR + 1) * HALF
ZX, ZX_GO, ZX_Y = 0, 256, 128
XZ, XZ_GO, XZ_Y = 384, 176, 80


def hop_order():
    offsets = [(dx, dz) for dx in (0, 1, -1, 2) for dz in (1, -1, 2, -2, 3, -3, 4, 0) if (dx, dz) != (0, 0)]
    return sorted(offsets, key=lambda o: (abs(o[0]) + abs(o[1]), abs(o[0])))


ORDER = hop_order()


def packed(i, values):
    words = [sum(v << (3 * k) for k, v in enumerate(values[w : w + 8])) for w in range(0, len(values), 8)]
    word = jnp.int32(words[0])
    for n, w in enumerate(words[1:], 1):
        word = jnp.where(i // 8 == n, jnp.int32(w), word)
    return (word >> (3 * (i % 8))) & 7


def kernel(
    cot_hbm, act_hbm, lens, cf_hbm, rf, tg_hbm, out,
    cot, act, masked, flipped, grads, big, acc, spread, part, part_in, tacc, halves, pay, land,
    lsem, ssem, msem, rzx, rxz, ryzx, ryxz,
):
    a, p = lax.axis_index("dp"), lax.axis_index("proj")
    y, c = a // 2, a % 2
    x, z = p // ZS, p % ZS
    odd = y % 2
    sib = (y * 2 + 1 - c, p)

    def at(ax, az):
        return (a, ((ax + XS) % XS) * ZS + (az + ZS) % ZS)

    def at_y(ay):
        return (((ay + YS) % YS) * 2 + c, p)

    bar = pltpu.get_barrier_semaphore()

    @pl.loop(1, NP)
    def _(i):
        pl.semaphore_signal(bar, inc=1, device_id=(a, (p + i) % NP), device_id_type=MESH)

    @pl.loop(1, 2 * YS)
    def _(i):
        pl.semaphore_signal(bar, inc=1, device_id=((a + i) % (2 * YS), p), device_id_type=MESH)

    own = []
    for g in range(GR):
        own.append(
            pltpu.make_async_copy(
                cf_hbm.at[g, pl.ds(pl.multiple_of(c * HALF, HALF), HALF)], big.at[p, pl.ds(g * HALF, HALF)], lsem.at[g]
            )
        )
    own_act = pltpu.make_async_copy(act_hbm, act, lsem.at[5])
    own_cot = pltpu.make_async_copy(cot_hbm, cot.at[pl.ds(c * E, E)], lsem.at[4])
    for copy in own:
        copy.start()
    own_act.start()
    own_cot.start()

    acc[...] = jnp.zeros_like(acc)
    tacc[...] = jnp.zeros_like(tacc)
    own_act.wait()
    tokens = lax.broadcasted_iota(jnp.int32, (TOK, RANK), 0)
    for e in range(E):
        kept = jnp.where(tokens < lens[e], act[e].astype(jnp.float32), 0.0)
        masked[c * E + e] = kept.astype(jnp.bfloat16)

    pl.semaphore_wait(bar, NP - 1 + 2 * YS - 1)

    def push(src, dst, s, r, to):
        pltpu.make_async_remote_copy(src_ref=src, dst_ref=dst, send_sem=s, recv_sem=r, device_id=to, device_id_type=MESH).start()

    def zx(j):
        return big.at[j, pl.ds(pl.multiple_of(ZX + ZX_Y * odd, 16), ZX_GO)]

    def xz(j):
        return big.at[j, pl.ds(pl.multiple_of(XZ + XZ_Y * odd, 16), XZ_GO)]

    def zx_y(j, plane):
        return big.at[j, pl.ds(pl.multiple_of(ZX + 256 * plane, 16), ZX_Y)]

    def xz_y(j, plane):
        return big.at[j, pl.ds(pl.multiple_of(XZ + 176 * plane, 16), XZ_Y)]

    def push_zx(j, to):
        push(zx(j), zx(j), ssem.at[0], rzx.at[j], to)

    def push_xz(j, to):
        push(xz(j), xz(j), ssem.at[1], rxz.at[j], to)

    def await_bytes(ref, sem):
        pltpu.make_async_copy(ref, ref, sem).wait()

    keeper = a // YS
    slot = big.at[p, pl.ds(pl.multiple_of(GR * HALF + 16 * (a % YS), 16), 16)]

    @pl.when(keeper == c)
    def _():
        pltpu.make_async_copy(tg_hbm, slot, msem.at[0]).start()

    @pl.when(keeper != c)
    def _():
        push(tg_hbm, slot, ssem.at[4], msem.at[0], sib)

    @pl.loop(1, YS)
    def _(i):
        push(tg_hbm, slot, ssem.at[4], msem.at[0], (((y + i) % YS) * 2 + keeper, p))

    for copy in own:
        copy.wait()
    for to in (at(x, z + 1), at(x, z - 1), at(x + 1, z), at(x - 1, z)):
        push_zx(p, to)

    mine, theirs = pl.ds(c * E, E), pl.ds((1 - c) * E, E)
    push(masked.at[mine], masked.at[mine], ssem.at[5], msem.at[1], sib)
    push(cot_hbm, cot.at[mine], ssem.at[6], msem.at[2], sib)

    await_bytes(big.at[p, pl.ds(GR * HALF, HALF)], msem.at[0])
    for to in (at(x + 1, z), at(x - 1, z), at(x, z + 1), at(x, z - 1)):
        push_xz(p, to)

    def candidate_grads(first):
        for e in range(E):
            flipped[first + e] = masked[first + e].astype(jnp.float32).T.astype(jnp.bfloat16)

        @pl.loop(0, E)
        def _(e):
            n = first + e
            left = flipped[n]
            row = pl.ds(pl.multiple_of(n * RS, RS), RS)

            @pl.loop(0, NP // 4)
            def _(q):
                for h in range(2):
                    pieces = [
                        cot[n, :, pl.ds(pl.multiple_of((4 * q + 2 * h + k) * 256 + c * HALF, HALF), HALF)] for k in range(2)
                    ]
                    right = jnp.concatenate(pieces, axis=1)
                    g_all = jnp.dot(left, right, preferred_element_type=jnp.float32).astype(jnp.bfloat16)
                    for g in range(GR):
                        grads[g, row, pl.ds(pl.multiple_of((4 * q + 2 * h) * HALF, 256), 256)] = g_all[g * RS : (g + 1) * RS]

    def block(j):
        columns = pl.ds(pl.multiple_of(j * HALF, HALF), HALF)
        for g in range(GR):
            acc[g] += jnp.dot(grads[g, :, columns], big[j, g * HALF : (g + 1) * HALF, :], preferred_element_type=jnp.float32)
        t = big[j, GR * HALF :, :].astype(jnp.float32)
        tacc[...] += t * t

    def offset(i):
        return packed(i, [o[0] + 1 for o in ORDER]) - 1, packed(i, [o[1] + 3 for o in ORDER]) - 3

    def source(i):
        dx, dz = offset(i)
        return dx, dz, (x - dx + XS) % XS, (z - dz + ZS) % ZS

    def hand_on(i):
        dx, dz, sx, sz = source(i)
        j = sx * ZS + sz
        step_z = jnp.where(dz > 0, 1, -1)
        far_z = jnp.abs(dz)
        to_y = 1 - 2 * ((sx + sz) % 2)

        await_bytes(zx(j), rzx.at[j])
        last_z = jnp.where(dz == 3, sz % 2 == 0, (dz == -3) & (sz % 2 == 1))

        @pl.when((dx == 0) & ((far_z < 3) | last_z))
        def _():
            push_zx(j, at(x, z + step_z))

        @pl.when(dx == 0)
        def _():
            push_zx(j, at(x + 1, z))
            push_zx(j, at(x - 1, z))

        @pl.when(((dx == 1) & (sz % 2 == 0)) | ((dx == -1) & (sz % 2 == 1)))
        def _():
            push_zx(j, at(x + dx, z))

        push(zx_y(j, odd), zx_y(j, odd), ssem.at[2], ryzx.at[j], at_y(y + to_y))

        await_bytes(xz(j), rxz.at[j])
        last_zx = jnp.where(dz == 3, sx % 2 == 0, (dz == -3) & (sx % 2 == 1))

        @pl.when((dz == 0) & (((dx == 1) & (sx % 2 == 0)) | ((dx == -1) & (sx % 2 == 1))))
        def _():
            push_xz(j, at(x + dx, z))

        @pl.when(dz == 0)
        def _():
            push_xz(j, at(x, z + 1))
            push_xz(j, at(x, z - 1))

        @pl.when((dz != 0) & ((far_z < 3) | last_zx))
        def _():
            push_xz(j, at(x, z + step_z))

        push(xz_y(j, odd), xz_y(j, odd), ssem.at[3], ryxz.at[j], at_y(y - to_y))

    def arrived_block(i):
        _, _, sx, sz = source(i)
        j = sx * ZS + sz
        await_bytes(zx_y(j, 1 - odd), ryzx.at[j])
        await_bytes(xz_y(j, 1 - odd), ryxz.at[j])
        block(j)

    own_cot.wait()
    candidate_grads(c * E)

    @pl.loop(0, 4)
    def _(i):
        hand_on(i)

    await_bytes(masked.at[theirs], msem.at[1])
    await_bytes(cot.at[theirs], msem.at[2])
    candidate_grads((1 - c) * E)
    block(p)

    big_rows = lax.broadcasted_iota(jnp.int32, (KR * 2 * E, KR), 0) // (2 * E)
    pick_k = (big_rows == lax.broadcasted_iota(jnp.int32, (KR * 2 * E, KR), 1)).astype(jnp.bfloat16)
    big_cols = lax.broadcasted_iota(jnp.int32, (RS, 2 * E * RS), 1) % RS
    pick_a = (big_cols == lax.broadcasted_iota(jnp.int32, (RS, 2 * E * RS), 0)).astype(jnp.bfloat16)
    same = lax.broadcasted_iota(jnp.int32, (256, 256), 0) % (2 * E) == lax.broadcasted_iota(jnp.int32, (256, 256), 1) // RS
    for g in range(GR):
        by_k = lax.dot_general(pick_k, rf[g], (((1,), (1,)), ((), ())), preferred_element_type=jnp.float32)
        wide = jnp.dot(by_k.astype(jnp.bfloat16), pick_a, preferred_element_type=jnp.float32)
        spread[g] = jnp.where(same, wide, 0.0).astype(jnp.bfloat16)

    def done_after(i):
        return jnp.maximum((i + 1) * 35 // 31 - 6, 0)

    @pl.loop(4, NP - 1)
    def _(i):
        hand_on(i)

        @pl.loop(done_after(i - 1), done_after(i))
        def _(k):
            arrived_block(k)

    @pl.loop(done_after(NP - 2), NP - 1)
    def _(k):
        arrived_block(k)

    total = jnp.zeros((KR * 2 * E, KC), jnp.float32)
    for g in range(GR):
        inner = acc[g]
        high = inner.astype(jnp.bfloat16)
        low = (inner - high.astype(jnp.float32)).astype(jnp.bfloat16)
        total += jnp.dot(spread[g], high, preferred_element_type=jnp.float32)
        total += jnp.dot(spread[g], low, preferred_element_type=jnp.float32)
    part[...] = total
    push(part, part_in, ssem.at[7], msem.at[3], sib)
    targ_sq = lax.dot_general(
        jnp.ones((2 * E, KC), jnp.float32), tacc[...], (((1,), (1,)), ((), ())),
        precision=lax.Precision.HIGHEST, preferred_element_type=jnp.float32,
    )
    await_bytes(part_in, msem.at[3])

    dots = jnp.zeros((4 * E, HALF), jnp.float32)
    squares = jnp.zeros((2 * E, KC), jnp.float32)
    for k in range(KR):
        feat = part[2 * E * k : 2 * E * (k + 1)] + part_in[2 * E * k : 2 * E * (k + 1)]
        squares += feat * feat
        high = feat.astype(jnp.bfloat16).astype(jnp.float32)
        both = jnp.concatenate([high, feat - high], axis=0).astype(jnp.bfloat16)
        dots += lax.dot_general(
            both, big[k, GR * HALF :, :], (((1,), (1,)), ((), ())), preferred_element_type=jnp.float32
        )
    cand_sq = jnp.sum(squares, axis=1, keepdims=True)
    product = dots[: 2 * E] + dots[2 * E :]
    scores = math.sqrt(KR * KC) * product / (jnp.sqrt(cand_sq + EPS) * jnp.sqrt(targ_sq + EPS))

    halves[c] = scores
    push(halves.at[c], halves.at[c], ssem.at[8], msem.at[4], sib)
    await_bytes(halves.at[1 - c], msem.at[4])
    for h in range(2):
        rows = halves[h]
        pay[E * h : E * (h + 1)] = jnp.where(c == 0, rows[:E], rows[E:])
    pltpu.make_async_copy(pay, land.at[p], msem.at[5]).start()

    @pl.loop(1, NP)
    def _(i):
        push(pay, land.at[p], ssem.at[9], msem.at[5], (a, (p + i) % NP))

    await_bytes(land, msem.at[5])
    for j in range(NP):
        for h in range(2):
            out[E * j : E * (j + 1), HALF * h : HALF * (h + 1)] = land[j, E * h : E * (h + 1)]

    rest = pl.ds(0, NP - 1)
    await_bytes(big.at[rest, pl.ds(0, ZX_GO)], ssem.at[0])
    await_bytes(big.at[rest, pl.ds(0, XZ_GO)], ssem.at[1])
    await_bytes(big.at[rest, pl.ds(0, ZX_Y)], ssem.at[2])
    await_bytes(big.at[rest, pl.ds(0, XZ_Y)], ssem.at[3])
    await_bytes(big.at[0, pl.ds(0, 16 * (YS - 1))], ssem.at[4])

    @pl.when(keeper != c)
    def _():
        await_bytes(big.at[0, pl.ds(0, 16)], ssem.at[4])

    await_bytes(masked.at[mine], ssem.at[5])
    await_bytes(cot.at[mine], ssem.at[6])
    await_bytes(part, ssem.at[7])
    await_bytes(halves.at[c], ssem.at[8])
    await_bytes(land.at[rest], ssem.at[9])


def on_device(cotangents, adapter_activations, lengths, column_factors, row_factors, targets):
    anywhere = pl.BlockSpec(memory_space=pl.ANY)
    vmem = pl.BlockSpec(memory_space=pltpu.VMEM)
    bf16, f32 = jnp.bfloat16, jnp.float32
    dma = pltpu.SemaphoreType.DMA
    return pl.pallas_call(
        kernel,
        out_shape=jax.ShapeDtypeStruct((NP * E, 2 * HALF), f32),
        in_specs=[anywhere, anywhere, pl.BlockSpec(memory_space=pltpu.SMEM), anywhere, vmem, anywhere],
        out_specs=vmem,
        scratch_shapes=[
            pltpu.VMEM((2 * E, TOK, NP * 256), bf16),
            pltpu.VMEM((E, TOK, RANK), bf16),
            pltpu.VMEM((2 * E, TOK, RANK), bf16),
            pltpu.VMEM((2 * E, RANK, TOK), bf16),
            pltpu.VMEM((GR, 2 * E * RS, NP * HALF), bf16),
            pltpu.VMEM((NP, ROWS, KC), bf16),
            pltpu.VMEM((GR, 2 * E * RS, KC), f32),
            pltpu.VMEM((GR, KR * 2 * E, 2 * E * RS), bf16),
            pltpu.VMEM((KR * 2 * E, KC), f32),
            pltpu.VMEM((KR * 2 * E, KC), f32),
            pltpu.VMEM((HALF, KC), f32),
            pltpu.VMEM((2, 2 * E, HALF), f32),
            pltpu.VMEM((2 * E, HALF), f32),
            pltpu.VMEM((NP, 2 * E, HALF), f32),
            dma((6,)),
            dma((10,)),
            dma((6,)),
            dma((NP,)),
            dma((NP,)),
            dma((NP,)),
            dma((NP,)),
        ],
        compiler_params=pltpu.CompilerParams(collective_id=0, has_side_effects=True, vmem_limit_bytes=56 * 2**20),
        cost_estimate=pl.CostEstimate(flops=3 * 10**9, bytes_accessed=6 * 2**20, transcendentals=0),
    )(cotangents, adapter_activations, lengths, column_factors, row_factors, targets)


def solution(mesh):
    placed = (
        P(("dp", "proj"), None, None),
        P(("dp", "proj"), None, None),
        P(("dp", "proj")),
        P(None, "proj", None),
        P(),
        P("dp", "proj"),
    )
    return jax.shard_map(on_device, mesh=mesh, in_specs=placed, out_specs=P("dp", None), check_vma=False)
```

time: 726 us -> 85.1 us (0.12)
  waiting for transfers between devices: 361 us -> 0 us
  blocking collectives: 277 us -> 0 us
  Pallas kernels: 0 us -> 83.3 us
  local copies, waits for them, and re-layouts: 39.5 us -> 1.57 us
  matrix products: 27.1 us -> 0 us
  between operations: 13.5 us -> 0.01 us
    reduce_scatter x1 -> x0, waiting for transfers between devices: 201 us -> none  [on_device(): lax.psum_scatter(partial_value, 'proj', scatter_dimension=1, tiled=True)]
    all_to_all x1 -> x0, blocking collectives: 196 us -> none  [on_device(): lax.all_to_all(grads, 'proj', split_axis=2, concat_axis=0, tiled=True)]
    psum x1 -> x0, waiting for transfers between devices: 161 us -> none  [on_device(): scores = math.sqrt(FEATURE_DIM) * lax.psum(dot_part, 'proj')]
    pallas_call x0 -> x1, Pallas kernels: none -> 83.3 us  [on_device(): pl.pallas_call(kernel, out_shape=jax.ShapeDtypeStruct((NP * E, 2 * HALF),...]
    psum x1 -> x0, blocking collectives: 58.1 us -> none  [on_device(): cand_sq, targ_sq = lax.psum((cand_part, targ_part), 'proj')]
    dot_general x10 -> x0, matrix products: 27.1 us -> none  [the longest x4 10.4 us: on_device(): jnp.einsum('ak,mac->mkc', row_f32[group], inner_terms, precision=lax.Prec...]
    all_gather x1 -> x0, blocking collectives: 22.7 us -> none  [on_device(): target_all = lax.all_gather(targets, 'dp', axis=0, tiled=True)]
    all_to_all x2 -> x0, local copies, waits for them, and re-layouts: 19.7 us -> none  [on_device(): lax.all_to_all(grads, 'proj', split_axis=2, concat_axis=0, tiled=True)]
  transfers between devices with their start and end apart: 2 -> 0, of which waited for: 2 -> 0; matrix products, arithmetic and copies ran while one was open for 0% -> 0% of each run, Pallas kernels for 0% -> 0%
where the time goes in v1:
time: 85.1 us; the launch traced here: 84.9 us
  Pallas kernels  83.3 us (98%)
  local copies, waits for them, and re-layouts  1.57 us (2%)
    pallas_call x1, Pallas kernels, on_device(): pl.pallas_call(kernel, out_shape=jax.ShapeDtypeStruct((NP * E, 2 * HALF),...  83.3 us

profile of v1, /device:TPU:1, one launch (start us, length us, event | category | flops | bytes accessed | tf_op | source)
XLA Modules:
  0.0 84.9 jit_solution(1889577481380198539)
XLA Ops:
  0.0 83.3 %shard_map.64 = f32[128,256]{1,0:T(8,128)} custom-call(bf16[4,64,8192]{2,1,0:T(8,128)(2,1)} %cot_hbm.1, bf16[4,64,128]{2,1,0:T(8,128)(2,1)} %act_hbm.1, s32[4]{0:T(128)} %lens.1, bf16[4,256,256]{2,1,0:T(8,128)(2,1)} %cf_hbm.1, bf16[4,32,32]{2,1,0:T(8,128)(2,1)} %rf.1, bf16[16,256]{1,0:T(8,128)(2,1)} %tg_hbm.1), custom_call_target="tpu_custom_call" | custom-call | flops 3000000000 | bytes 6291456 | tf_op jit(solution)/shard_map/pallas_call | solution.py:333
  83.3 1.6 %copy.8 = f32[128,256]{1,0:T(8,128)} copy(f32[128,256]{1,0:T(8,128)} %shard_map.64) | data formatting | bytes 262144

commit v2 on v1

v2 whole, which is shorter than its diff:
```python
import functools
import math

import jax
import jax.numpy as jnp
from jax import lax
from jax.experimental import pallas as pl
from jax.experimental.pallas import tpu as pltpu
from jax.sharding import PartitionSpec as P

MESH = pl.DeviceIdType.MESH
EPS = 1e-06
XS, YS, ZS = 4, 8, 8
NP = XS * ZS
GR, RS, KR, KC = 4, 32, 32, 256
E, TOK, RANK = 4, 64, 128
HALF = 128
ROWS = (GR + 1) * HALF
ZX, ZX_GO, ZX_Y = 0, 256, 128
XZ, XZ_GO, XZ_Y = 384, 176, 80


OFFSETS = sorted(
    [(dx, dz) for dx in (0, 1, -1, 2) for dz in (1, -1, 2, -2, 3, -3, 4, 0)], key=lambda o: abs(o[0]) + abs(o[1])
)
SCHEDULE = [
    ("zx", 0, 0, "z+"), ("zx", 0, 0, "x-"), ("zx", 0, 0, "x+"), ("zx", 0, 0, "z-"), ("mine", 0, 0, ""),
    ("xz", 0, 0, "x+"), ("xz", 0, 0, "z+"), ("xz", 0, 0, "x-"), ("xz", 0, 0, "z-"), ("zx", 0, 1, "z+"),
    ("zx", 0, -1, "z-"), ("zx", 0, -1, "x+"), ("zx", 0, -1, "x-"), ("zx", 1, 0, "y"), ("zx", -1, 0, "y"),
    ("zx", 0, 1, "y"), ("xz", 1, 0, "x+"), ("xz", -1, 0, "y"), ("xz", 0, -1, "z-"), ("zx", 0, 1, "x+"),
    ("xz", 1, 0, "z+"), ("xz", -1, 0, "x-"), ("zx", 0, 1, "x-"), ("xz", 0, -1, "y"), ("zx", -1, 0, "x-"),
    ("xz", -1, 0, "z-"), ("xz", 0, 1, "z+"), ("xz", 0, 1, "y"), ("zx", 1, -1, "y"), ("zx", 1, -1, "x+"),
    ("zx", 0, 2, "z+"), ("zx", 0, 2, "y"), ("zx", 0, -2, "x-"), ("zx", 0, -2, "y"), ("zx", -1, -1, "x-"),
    ("zx", 0, -2, "z-"), ("zx", 0, -1, "y"), ("xz", 2, 0, "z+"), ("xz", 1, 0, "y"), ("zx", -1, -1, "y"),
    ("zx", 0, -2, "x+"), ("xz", 2, 0, "z-"), ("xz", 2, 0, "y"), ("xz", 0, -2, "y"), ("xz", 1, 1, "y"),
    ("xz", -1, 0, "z+"), ("xz", 1, 0, "z-"), ("zx", 1, 0, "x+"), ("xz", -1, -1, "y"), ("theirs", 0, 0, ""),
    ("zx", 0, 3, "y"), ("zx", -1, 1, "y"), ("zx", 0, -3, "z-"), ("zx", 0, 3, "x-"), ("zx", 0, 3, "z+"),
    ("xz", 0, 2, "y"), ("zx", 0, -3, "x+"), ("xz", 2, 1, "y"), ("zx", 0, -3, "y"), ("zx", 0, 2, "x-"),
    ("zx", 1, 1, "y"), ("zx", 0, 2, "x+"), ("xz", -1, -1, "z-"), ("zx", -1, 1, "x-"), ("zx", 2, -1, "y"),
    ("xz", -1, 1, "z+"), ("zx", -1, -2, "y"), ("zx", 2, 0, "y"), ("xz", 2, 1, "z+"), ("zx", -1, -2, "x-"),
    ("zx", 1, -2, "y"), ("zx", 0, -3, "x-"), ("xz", 2, -1, "y"), ("xz", 0, -2, "z-"), ("zx", 1, -2, "x+"),
    ("zx", 1, -3, "y"), ("xz", -1, 1, "y"), ("zx", 1, 1, "x+"), ("zx", 0, 4, "y"), ("xz", 1, -1, "z-"),
    ("xz", 1, 1, "z+"), ("zx", 0, 4, "x-"), ("xz", 2, -1, "z-"), ("xz", -1, 2, "z+"), ("xz", 1, -1, "y"),
    ("zx", -1, 3, "y"), ("xz", -1, 2, "y"), ("zx", 1, 2, "y"), ("xz", 0, 2, "z+"), ("xz", -1, -2, "z-"),
    ("zx", 0, 4, "x+"), ("zx", 0, 3, "x+"), ("xz", -1, -2, "y"), ("xz", 2, 2, "z+"), ("xz", 0, -3, "y"),
    ("zx", -1, 2, "y"), ("xz", 2, 2, "y"), ("group", 1, 0, ""), ("zx", 2, 1, "y"), ("xz", 1, 2, "y"),
    ("zx", -1, 2, "x-"), ("group", 2, 0, ""), ("zx", 2, -2, "y"), ("xz", 1, -2, "z-"), ("xz", 2, -2, "y"),
    ("xz", 1, 2, "z+"), ("xz", 2, -2, "z-"), ("zx", 1, 4, "y"), ("zx", -1, -3, "x-"), ("xz", -1, 3, "y"),
    ("zx", 1, -3, "x+"), ("zx", -1, -3, "y"), ("xz", -1, 3, "z+"), ("xz", -1, -3, "z-"), ("zx", 1, 2, "x+"),
    ("xz", 1, -2, "y"), ("zx", -1, 3, "x-"), ("xz", 0, -3, "z-"), ("zx", -1, 4, "y"), ("zx", 1, 4, "x+"),
    ("zx", 1, 3, "x+"), ("xz", 0, 3, "z+"), ("zx", 1, 3, "y"), ("xz", 2, 3, "z+"), ("zx", -1, 4, "x-"),
    ("xz", 1, -3, "y"), ("xz", 0, 3, "y"), ("xz", 2, 3, "y"), ("group", 0, 0, ""), ("xz", 1, 3, "y"),
    ("xz", 2, -3, "z-"), ("zx", 2, 2, "y"), ("xz", 1, 3, "z+"), ("xz", 2, -3, "y"), ("zx", 2, -3, "y"),
    ("xz", 1, -3, "z-"), ("xz", -1, 4, "y"), ("xz", 0, 4, "y"), ("zx", 2, 3, "y"), ("zx", 2, 4, "y"),
    ("group", 3, 0, ""), ("xz", 2, 4, "y"), ("group", 4, 0, ""), ("xz", 1, 4, "y"), ("xz", -1, -3, "y"),
    ("group", 5, 0, ""), ("group", 7, 0, ""), ("group", 6, 0, ""),
]
GROUP = 4


def kernel(
    cot_hbm, act_hbm, lens, cf_hbm, rf, tg_hbm, out,
    cot, act, masked, flipped, grads, big, tgt_in, acc, spread, part, part_in, tacc, tsq, tsq_in, pay, land,
    lsem, ssem, msem, rzx, rxz, ryzx, ryxz,
):
    a, p = lax.axis_index("dp"), lax.axis_index("proj")
    y, c = a // 2, a % 2
    x, z = p // ZS, p % ZS
    odd = y % 2
    sib = (y * 2 + 1 - c, p)

    def at(ax, az):
        return (a, ((ax + XS) % XS) * ZS + (az + ZS) % ZS)

    def at_y(ay):
        return (((ay + YS) % YS) * 2 + c, p)

    own = []
    for g in range(GR):
        own.append(
            pltpu.make_async_copy(
                cf_hbm.at[g, pl.ds(pl.multiple_of(c * HALF, HALF), HALF)], big.at[p, pl.ds(g * HALF, HALF)], lsem.at[g]
            )
        )
    own_act = pltpu.make_async_copy(act_hbm, act, lsem.at[5])
    own_cot = pltpu.make_async_copy(cot_hbm, cot.at[pl.ds(c * E, E)], lsem.at[4])
    for copy in own:
        copy.start()

    bar = pltpu.get_barrier_semaphore()

    @pl.loop(1, NP)
    def _(i):
        pl.semaphore_signal(bar, inc=1, device_id=(a, (p + i) % NP), device_id_type=MESH)

    @pl.loop(1, 2 * YS)
    def _(i):
        pl.semaphore_signal(bar, inc=1, device_id=((a + i) % (2 * YS), p), device_id_type=MESH)

    own_act.start()
    own_cot.start()
    for copy in own:
        copy.wait()
    pl.semaphore_wait(bar, NP - 1 + 2 * YS - 1)

    def push(src, dst, s, r, to):
        pltpu.make_async_remote_copy(src_ref=src, dst_ref=dst, send_sem=s, recv_sem=r, device_id=to, device_id_type=MESH).start()

    def zx(j):
        return big.at[j, pl.ds(pl.multiple_of(ZX + ZX_Y * odd, 16), ZX_GO)]

    def xz(j):
        return big.at[j, pl.ds(pl.multiple_of(XZ + XZ_Y * odd, 16), XZ_GO)]

    def zx_y(j, plane):
        return big.at[j, pl.ds(pl.multiple_of(ZX + ZX_GO * plane, 16), ZX_Y)]

    def xz_y(j, plane):
        return big.at[j, pl.ds(pl.multiple_of(XZ + XZ_GO * plane, 16), XZ_Y)]

    def push_zx(j, to):
        push(zx(j), zx(j), ssem.at[0], rzx.at[j], to)

    def push_xz(j, to):
        push(xz(j), xz(j), ssem.at[1], rxz.at[j], to)

    def await_bytes(ref, sem):
        pltpu.make_async_copy(ref, ref, sem).wait()

    keeper = a // YS
    slot = big.at[p, pl.ds(pl.multiple_of(GR * HALF + 16 * (a % YS), 16), 16)]

    @pl.when(keeper == c)
    def _():
        pltpu.make_async_copy(tg_hbm, slot, msem.at[0]).start()

    @pl.when(keeper != c)
    def _():
        push(tg_hbm, slot, ssem.at[4], msem.at[0], sib)

    @pl.loop(1, YS)
    def _(i):
        push(tg_hbm, slot, ssem.at[4], msem.at[0], (((y + i) % YS) * 2 + keeper, p))

    def candidate_grads(first):
        for e in range(E):
            flipped[first + e] = masked[first + e].astype(jnp.float32).T.astype(jnp.bfloat16)

        @pl.loop(0, E)
        def _(e):
            n = first + e
            row = pl.ds(pl.multiple_of(n * RS, RS), RS)
            for h in range(2):
                half = NP // 2
                pieces = [
                    cot[n, :, pl.ds(pl.multiple_of((h * half + k) * 256 + c * HALF, HALF), HALF)] for k in range(half)
                ]
                right = jnp.concatenate(pieces, axis=1)
                g_all = jnp.dot(flipped[n], right, preferred_element_type=jnp.float32).astype(jnp.bfloat16)
                for g in range(GR):
                    grads[g, row, h * half * HALF : (h + 1) * half * HALF] = g_all[g * RS : (g + 1) * RS]

    def source(dx, dz):
        sx, sz = (x - dx + XS) % XS, (z - dz + ZS) % ZS
        return sx, sz, sx * ZS + sz

    mine, theirs = pl.ds(c * E, E), pl.ds((1 - c) * E, E)

    def share_candidates():
        push(cot_hbm, cot.at[mine], ssem.at[6], msem.at[2], sib)
        own_act.wait()
        tokens = lax.broadcasted_iota(jnp.int32, (TOK, RANK), 0)
        for e in range(E):
            kept = jnp.where(tokens < lens[e], act[e].astype(jnp.float32), 0.0)
            masked[c * E + e] = kept.astype(jnp.bfloat16)
        push(masked.at[mine], masked.at[mine], ssem.at[5], msem.at[1], sib)

    held = set()

    def send(tree, dx, dz, way):
        sx, sz, j = source(dx, dz)
        if (tree, dx, dz) not in held:
            held.add((tree, dx, dz))
            if (dx, dz) != (0, 0):
                await_bytes(zx(j) if tree == "zx" else xz(j), (rzx if tree == "zx" else rxz).at[j])
            elif tree == "xz":
                await_bytes(big.at[p, pl.ds(GR * HALF, HALF)], msem.at[0])
        if way == "y":
            to_y = 1 - 2 * ((sx + sz) % 2)
            if tree == "zx":
                push(zx_y(j, odd), zx_y(j, odd), ssem.at[2], ryzx.at[j], at_y(y + to_y))
            else:
                push(xz_y(j, odd), xz_y(j, odd), ssem.at[3], ryxz.at[j], at_y(y - to_y))
            return
        step = 1 if way[1] == "+" else -1
        to = at(x + step, z) if way[0] == "x" else at(x, z + step)

        def go():
            (push_zx if tree == "zx" else push_xz)(j, to)

        if way[0] == "z" and abs(dz) == 3:
            pl.when((sz if tree == "zx" else sx) % 2 == (0 if dz > 0 else 1))(go)
        elif way[0] == "x" and abs(dx) == 1:
            pl.when((sz if tree == "zx" else sx) % 2 == (0 if dx > 0 else 1))(go)
        else:
            go()

    def multiply(offsets):
        js = [source(dx, dz)[2] for dx, dz in offsets]
        for (dx, dz), j in zip(offsets, js):
            if (dx, dz) != (0, 0):
                await_bytes(zx_y(j, 1 - odd), ryzx.at[j])
                await_bytes(xz_y(j, 1 - odd), ryxz.at[j])
            push(big.at[j, pl.ds(GR * HALF, HALF)], tgt_in.at[j], ssem.at[8], msem.at[4], sib)
        for g in range(GR):
            left = jnp.concatenate([grads[g, :, pl.ds(pl.multiple_of(j * HALF, HALF), HALF)] for j in js], axis=1)
            right = jnp.concatenate([big[j, g * HALF : (g + 1) * HALF, :] for j in js], axis=0)
            acc[g] += jnp.dot(left, right, preferred_element_type=jnp.float32)
        squares = tacc[...]
        for j in js:
            t = big[j, GR * HALF :, :].astype(jnp.float32)
            squares += t * t
        tacc[...] = squares

    def prepare():
        acc[...] = jnp.zeros_like(acc)
        tacc[...] = jnp.zeros_like(tacc)
        by_row = lax.broadcasted_iota(jnp.int32, (2 * KR * E, KR), 0) % (KR * E) // E
        pick_k = (by_row == lax.broadcasted_iota(jnp.int32, (2 * KR * E, KR), 1)).astype(jnp.bfloat16)
        by_col = lax.broadcasted_iota(jnp.int32, (RS, 2 * E * RS), 1) % RS
        pick_a = (by_col == lax.broadcasted_iota(jnp.int32, (RS, 2 * E * RS), 0)).astype(jnp.bfloat16)
        row = lax.broadcasted_iota(jnp.int32, (256, 256), 0)
        col = lax.broadcasted_iota(jnp.int32, (256, 256), 1) // RS
        same = row // (KR * E) * E + row % E == col
        for g in range(GR):
            by_k = lax.dot_general(pick_k, rf[g], (((1,), (1,)), ((), ())), preferred_element_type=jnp.float32)
            wide = jnp.dot(by_k.astype(jnp.bfloat16), pick_a, preferred_element_type=jnp.float32)
            spread[g] = jnp.where(same, wide, 0.0).astype(jnp.bfloat16)

    for n, (what, i, k, way) in enumerate(SCHEDULE):
        if what == "mine":
            own_cot.wait()
            candidate_grads(c * E)
        elif what == "theirs":
            await_bytes(masked.at[theirs], msem.at[1])
            await_bytes(cot.at[theirs], msem.at[2])
            candidate_grads((1 - c) * E)
            prepare()
        elif what == "group":
            multiply(OFFSETS[GROUP * i : GROUP * (i + 1)])
        else:
            send(what, i, k, way)
        if n == 3:
            share_candidates()

    total = jnp.zeros((2 * KR * E, KC), jnp.float32)
    for g in range(GR):
        inner = acc[g]
        high = inner.astype(jnp.bfloat16)
        low = (inner - high.astype(jnp.float32)).astype(jnp.bfloat16)
        total += jnp.dot(spread[g], high, preferred_element_type=jnp.float32)
        total += jnp.dot(spread[g], low, preferred_element_type=jnp.float32)
    part[...] = total.reshape(2, KR * E, KC)
    push(part.at[1 - c], part_in, ssem.at[7], msem.at[3], sib)
    tsq[...] = lax.dot_general(
        jnp.ones((2 * E, KC), jnp.float32), tacc[...], (((1,), (1,)), ((), ())),
        precision=lax.Precision.HIGHEST, preferred_element_type=jnp.float32,
    )
    push(tsq, tsq_in, ssem.at[10], msem.at[6], sib)
    await_bytes(tgt_in, msem.at[4])
    await_bytes(tsq_in, msem.at[6])
    await_bytes(part_in, msem.at[3])

    dots = [[jnp.zeros((4 * E, HALF), jnp.float32) for _ in range(2)] for _ in range(2)]
    squares = jnp.zeros((2 * E, KC), jnp.float32)
    for m in range(KR // 2):
        rows = slice(2 * E * m, 2 * E * (m + 1))
        feat = part[c, rows] + part_in[rows]
        squares += feat * feat
        high = feat.astype(jnp.bfloat16).astype(jnp.float32)
        both = jnp.concatenate([high, feat - high], axis=0).astype(jnp.bfloat16)
        for k in range(2):
            for h, t in enumerate((big[2 * m + k, GR * HALF :, :], tgt_in[2 * m + k])):
                dots[h][k] += lax.dot_general(both, t, (((1,), (1,)), ((), ())), preferred_element_type=jnp.float32)
    sums = jnp.sum(squares, axis=1, keepdims=True)
    cand_norm = jnp.sqrt(sums[:E] + sums[E:] + EPS)
    scores = []
    for h, t in enumerate((tsq, tsq_in)):
        even, late = dots[h]
        product = (even[:E] + even[2 * E : 3 * E]) + (late[E : 2 * E] + late[3 * E :])
        scores.append(math.sqrt(KR * KC) * product / (cand_norm * jnp.sqrt(t[:E] + EPS)))
    pay[:E] = jnp.where(c == 0, scores[0], scores[1])
    pay[E:] = jnp.where(c == 0, scores[1], scores[0])
    pltpu.make_async_copy(pay, land.at[p], msem.at[5]).start()

    @pl.loop(1, NP)
    def _(i):
        push(pay, land.at[p], ssem.at[9], msem.at[5], (a, (p + i) % NP))

    await_bytes(land, msem.at[5])
    for j in range(NP):
        for h in range(2):
            out[E * j : E * (j + 1), HALF * h : HALF * (h + 1)] = land[j, E * h : E * (h + 1)]

    rest = pl.ds(0, NP - 1)
    await_bytes(big.at[rest, pl.ds(0, ZX_GO)], ssem.at[0])
    await_bytes(big.at[rest, pl.ds(0, XZ_GO)], ssem.at[1])
    await_bytes(big.at[rest, pl.ds(0, ZX_Y)], ssem.at[2])
    await_bytes(big.at[rest, pl.ds(0, XZ_Y)], ssem.at[3])
    await_bytes(big.at[0, pl.ds(0, 16 * (YS - 1))], ssem.at[4])

    @pl.when(keeper != c)
    def _():
        await_bytes(big.at[0, pl.ds(0, 16)], ssem.at[4])

    await_bytes(masked.at[mine], ssem.at[5])
    await_bytes(cot.at[mine], ssem.at[6])
    await_bytes(part_in, ssem.at[7])
    await_bytes(tgt_in, ssem.at[8])
    await_bytes(land.at[rest], ssem.at[9])
    await_bytes(tsq, ssem.at[10])


def on_device(cotangents, adapter_activations, lengths, column_factors, row_factors, targets):
    anywhere = pl.BlockSpec(memory_space=pl.ANY)
    vmem = pl.BlockSpec(memory_space=pltpu.VMEM)
    bf16, f32 = jnp.bfloat16, jnp.float32
    dma = pltpu.SemaphoreType.DMA
    return pl.pallas_call(
        kernel,
        out_shape=jax.ShapeDtypeStruct((NP * E, 2 * HALF), f32),
        in_specs=[anywhere, anywhere, pl.BlockSpec(memory_space=pltpu.SMEM), anywhere, vmem, anywhere],
        out_specs=vmem,
        scratch_shapes=[
            pltpu.VMEM((2 * E, TOK, NP * 256), bf16),
            pltpu.VMEM((E, TOK, RANK), bf16),
            pltpu.VMEM((2 * E, TOK, RANK), bf16),
            pltpu.VMEM((2 * E, RANK, TOK), bf16),
            pltpu.VMEM((GR, 2 * E * RS, NP * HALF), bf16),
            pltpu.VMEM((NP, ROWS, KC), bf16),
            pltpu.VMEM((NP, HALF, KC), bf16),
            pltpu.VMEM((GR, 2 * E * RS, KC), f32),
            pltpu.VMEM((GR, KR * 2 * E, 2 * E * RS), bf16),
            pltpu.VMEM((2, KR * E, KC), f32),
            pltpu.VMEM((KR * E, KC), f32),
            pltpu.VMEM((HALF, KC), f32),
            pltpu.VMEM((2 * E, HALF), f32),
            pltpu.VMEM((2 * E, HALF), f32),
            pltpu.VMEM((2 * E, HALF), f32),
            pltpu.VMEM((NP, 2 * E, HALF), f32),
            dma((6,)),
            dma((11,)),
            dma((7,)),
            dma((NP,)),
            dma((NP,)),
            dma((NP,)),
            dma((NP,)),
        ],
        compiler_params=pltpu.CompilerParams(collective_id=0, has_side_effects=True, vmem_limit_bytes=56 * 2**20),
        cost_estimate=pl.CostEstimate(flops=3 * 10**9, bytes_accessed=6 * 2**20, transcendentals=0),
    )(cotangents, adapter_activations, lengths, column_factors, row_factors, targets)


def solution(mesh):
    placed = (
        P(("dp", "proj"), None, None),
        P(("dp", "proj"), None, None),
        P(("dp", "proj")),
        P(None, "proj", None),
        P(),
        P("dp", "proj"),
    )
    return jax.shard_map(on_device, mesh=mesh, in_specs=placed, out_specs=P("dp", None), check_vma=False)
```

time: 85.1 us -> 79.5 us (0.934)
  Pallas kernels: 83.3 us -> 77.7 us
    pallas_call x1, Pallas kernels: 83.3 us -> 77.7 us  [on_device(): pl.pallas_call(kernel, out_shape=jax.ShapeDtypeStruct((NP * E, 2 * HALF),...]
where the time goes in v2:
time: 79.5 us; the launch traced here: 79.3 us
  Pallas kernels  77.7 us (98%)
  local copies, waits for them, and re-layouts  1.57 us (2%)
    pallas_call x1, Pallas kernels, on_device(): pl.pallas_call(kernel, out_shape=jax.ShapeDtypeStruct((NP * E, 2 * HALF),...  77.7 us

profile of v2, /device:TPU:1, one launch (start us, length us, event | category | flops | bytes accessed | tf_op | source)
XLA Modules:
  0.0 79.3 jit_solution(2091560875897966098)
XLA Ops:
  0.0 77.7 %shard_map.64 = f32[128,256]{1,0:T(8,128)} custom-call(bf16[4,64,8192]{2,1,0:T(8,128)(2,1)} %cot_hbm.1, bf16[4,64,128]{2,1,0:T(8,128)(2,1)} %act_hbm.1, s32[4]{0:T(128)} %lens.1, bf16[4,256,256]{2,1,0:T(8,128)(2,1)} %cf_hbm.1, bf16[4,32,32]{2,1,0:T(8,128)(2,1)} %rf.1, bf16[16,256]{1,0:T(8,128)(2,1)} %tg_hbm.1), custom_call_target="tpu_custom_call" | custom-call | flops 3000000000 | bytes 6291456 | tf_op jit(solution)/shard_map/pallas_call | solution.py:329
  77.7 1.6 %copy.8 = f32[128,256]{1,0:T(8,128)} copy(f32[128,256]{1,0:T(8,128)} %shard_map.64) | data formatting | bytes 262144

commit v3 on v2

v3 whole, which is shorter than its diff:
```python
import functools
import math

import jax
import jax.numpy as jnp
from jax import lax
from jax.experimental import pallas as pl
from jax.experimental.pallas import tpu as pltpu
from jax.sharding import PartitionSpec as P

MESH = pl.DeviceIdType.MESH
EPS = 1e-06
XS, YS, ZS = 4, 8, 8
NP = XS * ZS
GR, RS, KR, KC = 4, 32, 32, 256
E, TOK, RANK = 4, 64, 128
HALF = 128
NB = NP // 2
ZX_ROWS = 336
XZ_ROWS = GR * HALF - ZX_ROWS
T_GO, T_Y = 80, 48


OFFSETS = sorted(
    [(dx, dz) for dx in (0, 1, -1, 2) for dz in (1, -1, 2, -2, 3, -3, 4, 0)], key=lambda o: abs(o[0]) + abs(o[1])
)
BY_PARITY = [[o for o in OFFSETS if sum(o) % 2 == parity] for parity in range(2)]
GROUP = 4
SCHEDULE = [
    (0, 0, 0, 0, "z-"), (1, 1, 0, 0, "x+"), (0, 0, 0, 0, "z+"), (1, 1, 0, 0, "x-"), (12, 0, 0, 0, ""), (2, 0, 0, 0, "z+"),
    (2, 0, 0, 0, "x-"), (2, 0, 0, 0, "z-"), (2, 0, 0, 0, "x+"), (2, 1, 0, 0, "x+"), (1, 1, -1, 0, "x-"), (1, 1, -1, 0, "z-"),
    (1, 1, 0, 0, "z-"), (1, 1, -1, 0, "z+"), (1, 1, 0, 0, "z+"), (1, 1, 1, 0, "x+"), (0, 0, 0, 0, "x-"), (2, 1, 0, 0, "z-"),
    (2, 1, 0, 0, "z+"), (2, 0, 0, 1, "z+"), (2, 0, 0, -1, "x+"), (2, 0, 0, 1, "x+"), (0, 0, 0, 1, "x+"), (2, 0, 0, -1, "x-"),
    (0, 0, 0, -1, "z-"), (0, 0, 0, -1, "x-"), (0, 0, 0, -1, "x+"), (0, 0, 0, 0, "x+"), (0, 0, 0, 1, "z+"), (2, 0, 0, -1, "z-"),
    (2, 0, 0, 2, "z+"), (2, 1, 0, 0, "x-"), (0, 0, 0, 1, "x-"), (2, 1, 0, 1, "z+"), (2, 1, 1, 0, "x+"), (2, 1, 1, 0, "z+"),
    (2, 1, 1, 0, "z-"), (1, 1, 2, 0, "z-"), (2, 0, 0, -2, "z-"), (2, 0, 0, 1, "x-"), (1, 1, 2, 0, "z+"), (0, 0, 0, 2, "x-"),
    (0, 0, 0, 2, "z+"), (0, 0, 0, -2, "z-"), (0, 0, 0, 2, "x+"), (2, 1, -1, 0, "z-"), (2, 0, 0, -3, "z-"), (2, 0, 0, 2, "x-"),
    (2, 0, 0, 2, "x+"), (0, 0, 0, -2, "x-"), (2, 1, -1, 0, "x-"), (2, 0, 0, 3, "x-"), (2, 0, 1, 1, "x+"), (2, 0, 0, 3, "x+"),
    (0, 0, 0, -2, "x+"), (2, 1, -1, 0, "z+"), (2, 0, 0, -2, "x+"), (1, 1, 0, -1, "z-"), (2, 1, 1, -1, "z-"), (1, 1, 1, 0, "z-"),
    (2, 0, -1, -1, "x-"), (2, 0, 0, -3, "x-"), (2, 0, 0, -2, "x-"), (1, 1, 0, 1, "z+"), (0, 0, 1, 0, "x+"), (2, 0, 1, -1, "x+"),
    (1, 1, -1, 1, "z+"), (2, 1, -1, -1, "z-"), (2, 0, -1, 2, "x-"), (2, 0, 1, 2, "x+"), (1, 1, -1, -1, "z-"), (1, 1, 1, 0, "z+"),
    (2, 0, 0, 3, "z+"), (2, 0, -1, 1, "x-"), (1, 1, 2, 1, "z+"), (2, 1, -1, 1, "z+"), (2, 1, 2, 0, "z-"), (2, 0, 0, -3, "x+"),
    (2, 1, 2, 0, "z+"), (1, 1, 2, -1, "z-"), (0, 0, 0, 3, "z+"), (0, 0, 0, -3, "x-"), (0, 0, 0, -3, "x+"), (0, 0, 1, 1, "x+"),
    (0, 0, 0, -3, "z-"), (0, 0, 0, 3, "x-"), (0, 0, -1, 0, "x-"), (2, 0, -1, 1, "y"), (12, 1, 0, 0, ""), (1, 1, 1, -1, "z-"),
    (1, 1, 1, 1, "z+"), (2, 0, -1, -2, "y"), (2, 0, 0, -1, "y"), (0, 0, 1, -1, "x+"), (2, 1, 1, -2, "z-"), (2, 0, 1, -2, "x+"),
    (0, 0, 0, 3, "x+"), (2, 1, 1, 1, "z+"), (2, 1, 2, 1, "z+"), (2, 1, 0, -1, "z-"), (2, 0, 1, -1, "y"), (2, 0, 0, 4, "x+"),
    (1, 1, -1, 2, "z+"), (2, 1, -1, -2, "z-"), (0, 0, -1, 1, "x-"), (2, 1, 2, -1, "z-"), (1, 1, 0, 2, "z+"), (0, 0, 1, -2, "x+"),
    (0, 0, -1, 2, "x-"), (1, 1, 0, -2, "z-"), (2, 0, -1, 2, "y"), (2, 1, 0, 2, "z+"), (2, 1, -1, 2, "z+"), (0, 0, -1, -1, "x-"),
    (0, 0, 0, 4, "x+"), (0, 0, 0, 4, "x-"), (2, 0, 1, -3, "x+"), (2, 1, 1, -3, "z-"), (2, 0, 2, 1, "y"), (2, 0, 1, 3, "x+"),
    (2, 0, -1, 0, "x-"), (2, 0, -1, -3, "x-"), (2, 0, -1, 3, "x-"), (1, 1, -1, -2, "z-"), (2, 0, 1, -3, "y"), (1, 1, 1, -2, "z-"),
    (1, 1, 2, 2, "z+"), (2, 1, 1, 2, "z+"), (2, 1, 0, -2, "z-"), (2, 0, 1, 0, "y"), (2, 0, 1, 0, "x+"), (1, 1, 2, -2, "z-"),
    (2, 0, 0, 4, "x-"), (1, 1, 1, 2, "z+"), (12, 2, 0, 0, ""), (2, 0, -1, -3, "y"), (2, 0, 2, 2, "y"), (2, 1, 2, -2, "z-"),
    (2, 1, -1, -3, "z-"), (2, 0, -1, -2, "x-"), (0, 0, -1, 3, "x-"), (2, 0, 2, -1, "y"), (0, 0, 1, -3, "x+"), (2, 1, 1, 3, "z+"),
    (1, 1, 0, 3, "z+"), (2, 0, -1, 3, "y"), (2, 1, -1, 3, "z+"), (0, 0, 1, 2, "x+"), (0, 0, -1, -2, "x-"), (1, 1, 0, -3, "z-"),
    (0, 0, 1, 4, "x+"), (0, 0, -1, -3, "x-"), (2, 1, 2, 2, "z+"), (1, 1, -1, -3, "z-"), (1, 1, -1, 3, "z+"), (1, 1, 2, 3, "z+"),
    (2, 0, 0, 1, "y"), (0, 0, 1, 3, "x+"), (2, 1, 0, 3, "z+"), (2, 1, 0, -3, "z-"), (0, 0, -1, 4, "x-"), (2, 0, 1, 1, "y"),
    (14, 0, 0, 0, ""), (1, 1, 1, -3, "z-"), (1, 1, 1, 3, "z+"), (13, 1, 0, 0, ""), (2, 0, 0, 2, "y"), (2, 0, 1, -2, "y"),
    (1, 1, 2, -3, "z-"), (2, 0, 0, 3, "y"), (2, 0, -1, 4, "x-"), (13, 0, 0, 0, ""), (2, 0, -1, -1, "y"), (2, 0, 1, 4, "x+"),
    (2, 0, 2, -3, "y"), (2, 0, 2, 3, "y"), (14, 1, 0, 0, ""), (2, 1, 2, -3, "z-"), (2, 0, 0, -3, "y"), (2, 0, 0, -2, "y"),
    (2, 0, 1, 4, "y"), (2, 1, 2, 3, "z+"), (2, 0, -1, 4, "y"), (14, 2, 0, 0, ""), (2, 0, 2, -2, "y"), (2, 0, 1, 3, "y"),
    (13, 2, 0, 0, ""), (2, 0, 0, 4, "y"), (2, 0, 2, 0, "y"), (2, 0, -1, 0, "y"), (2, 0, 1, 2, "y"), (13, 3, 0, 0, ""),
    (14, 3, 0, 0, ""), (2, 0, 2, 4, "y"), (16, 0, 0, 0, ""), (15, 2, 0, 0, ""), (15, 3, 0, 0, ""), (15, 0, 0, 0, ""),
    (15, 1, 0, 0, ""),
]


def kernel(
    cot_hbm, act_hbm, lens, cf_hbm, rf, tg_hbm, out,
    cot, act, masked, flipped, grads, big, tgt, tgt_in, acc, spread, part, part_in, tacc, tsq, tsq_in, pay, land,
    lsem, ssem, msem, csem, rzx, rxz, rt, rty,
):
    a, p = lax.axis_index("dp"), lax.axis_index("proj")
    y, c = a // 2, a % 2
    x, z = p // ZS, p % ZS
    odd = y % 2
    outside = (x + z + odd) % 2
    sib = (y * 2 + 1 - c, p)

    def at(ax, az):
        return (a, ((ax + XS) % XS) * ZS + (az + ZS) % ZS)

    def at_y(ay, core):
        return (((ay + YS) % YS) * 2 + core, p)

    def partner_y(core):
        return y + (1 - 2 * odd) * (1 - 2 * core)

    def push(src, dst, s, r, to):
        pltpu.make_async_remote_copy(src_ref=src, dst_ref=dst, send_sem=s, recv_sem=r, device_id=to, device_id_type=MESH).start()

    def await_bytes(ref, sem):
        pltpu.make_async_copy(ref, ref, sem).wait()

    def cot_columns(q, parity, half):
        sx = q // 4
        j = sx * ZS + 2 * (q % 4) + (sx + parity) % 2
        return cot_hbm.at[:, :, pl.ds(pl.multiple_of(j * 256 + half * HALF, HALF), HALF)]

    def cot_slot(who, q):
        return cot.at[who, :, :, pl.ds(pl.multiple_of(q * HALF, HALF), HALF)]

    own = []
    for g in range(GR):
        own.append(
            pltpu.make_async_copy(
                cf_hbm.at[g, pl.ds(pl.multiple_of(c * HALF, HALF), HALF)], big.at[p // 2, pl.ds(g * HALF, HALF)], lsem.at[g]
            )
        )
    own_act = pltpu.make_async_copy(act_hbm, act, lsem.at[5])

    @pl.when(outside == 0)
    def _():
        for copy in own:
            copy.start()

    bar = pltpu.get_barrier_semaphore()

    @pl.loop(1, NP)
    def _(i):
        pl.semaphore_signal(bar, inc=1, device_id=(a, (p + i) % NP), device_id_type=MESH)

    @pl.loop(1, 2 * YS)
    def _(i):
        pl.semaphore_signal(bar, inc=1, device_id=((a + i) % (2 * YS), p), device_id_type=MESH)

    own_act.start()

    @pl.loop(0, NB)
    def _(q):
        pltpu.make_async_copy(cot_columns(q, odd, c), cot_slot(c, q), lsem.at[4]).start()

    @pl.when(outside == 0)
    def _():
        for copy in own:
            copy.wait()

    pl.semaphore_wait(bar, NP - 1 + 2 * YS - 1)

    keeper = a // YS
    slot = tgt.at[p, pl.ds(pl.multiple_of(16 * (a % YS), 16), 16)]

    @pl.when(keeper == c)
    def _():
        pltpu.make_async_copy(tg_hbm, slot, msem.at[0]).start()

    @pl.when(keeper != c)
    def _():
        push(tg_hbm, slot, ssem.at[4], msem.at[0], sib)

    @pl.loop(1, YS)
    def _(i):
        push(tg_hbm, slot, ssem.at[4], msem.at[0], at_y(y + i, keeper))

    def zx(j):
        return big.at[j // 2, pl.ds(0, ZX_ROWS)]

    def xz(j):
        return big.at[j // 2, pl.ds(ZX_ROWS, XZ_ROWS)]

    def t_go(j):
        return tgt.at[j, pl.ds(pl.multiple_of(T_Y * odd, 16), T_GO)]

    def t_y(j, plane):
        return tgt.at[j, pl.ds(pl.multiple_of(T_GO * plane, 16), T_Y)]

    PARTS = ((zx, rzx), (xz, rxz), (t_go, rt))

    def source(dx, dz):
        sx, sz = (x - dx + XS) % XS, (z - dz + ZS) % ZS
        return sx, sz, sx * ZS + sz

    def share_candidates():
        own_act.wait()
        tokens = lax.broadcasted_iota(jnp.int32, (TOK, RANK), 0)
        for e in range(E):
            kept = jnp.where(tokens < lens[e], act[e].astype(jnp.float32), 0.0)
            masked[c, e] = kept.astype(jnp.bfloat16)
        for h in range(2):
            push(masked.at[c], masked.at[2 + c], ssem.at[5], msem.at[1 + c], at_y(partner_y(h), h))

        @pl.loop(0, NB)
        def _(q):
            for h in range(2):
                push(cot_columns(q, 1 - odd, h), cot_slot(2 + c, q), ssem.at[6], csem.at[2 + c], at_y(partner_y(h), h))

        push(masked.at[c], masked.at[c], ssem.at[5], msem.at[7], sib)

        @pl.loop(0, NB)
        def _(q):
            push(cot_columns(q, odd, 1 - c), cot_slot(c, q), ssem.at[6], csem.at[0], sib)

    def candidate_grads(who):
        for e in range(E):
            flipped[who, e] = masked[who, e].astype(jnp.float32).T.astype(jnp.bfloat16)

        @pl.loop(0, E)
        def _(e):
            row = pl.ds(pl.multiple_of((who * E + e) * RS, RS), RS)
            g_all = jnp.dot(flipped[who, e], cot[who, e], preferred_element_type=jnp.float32).astype(jnp.bfloat16)
            for g in range(GR):
                grads[g, row, :] = g_all[g * RS : (g + 1) * RS]

    def prepare():
        acc[...] = jnp.zeros_like(acc)
        tacc[...] = jnp.zeros_like(tacc)
        by_row = lax.broadcasted_iota(jnp.int32, (2 * KR * E, KR), 0) % (KR * E) // E
        pick_k = (by_row == lax.broadcasted_iota(jnp.int32, (2 * KR * E, KR), 1)).astype(jnp.bfloat16)
        by_col = lax.broadcasted_iota(jnp.int32, (RS, 2 * E * RS), 1) % RS
        pick_a = (by_col == lax.broadcasted_iota(jnp.int32, (RS, 2 * E * RS), 0)).astype(jnp.bfloat16)
        row = lax.broadcasted_iota(jnp.int32, (256, 256), 0)
        col = lax.broadcasted_iota(jnp.int32, (256, 256), 1) // RS
        same = row // (KR * E) * E + row % E == col
        for g in range(GR):
            by_k = lax.dot_general(pick_k, rf[g], (((1,), (1,)), ((), ())), preferred_element_type=jnp.float32)
            wide = jnp.dot(by_k.astype(jnp.bfloat16), pick_a, preferred_element_type=jnp.float32)
            spread[g] = jnp.where(same, wide, 0.0).astype(jnp.bfloat16)

    held = set()
    sent = [jnp.int32(0)] * 3

    def await_part(stream, dx, dz, parities):
        new = [r for r in parities if (stream, dx, dz, r) not in held]
        held.update((stream, dx, dz, r) for r in new)
        if not new or (dx, dz) == (0, 0) and stream < 2:
            return
        view, sems = PARTS[stream]
        j = source(dx, dz)[2]

        def go():
            if (dx, dz) == (0, 0):
                await_bytes(tgt.at[p], msem.at[0])
            else:
                await_bytes(view(j), sems.at[j])

        if len(new) == 2:
            go()
        else:
            pl.when((dx + dz + outside) % 2 == new[0])(go)

    def send(stream, tree, dx, dz, way):
        sx, sz, j = source(dx, dz)
        view, sems = PARTS[stream]
        if way == "y":
            await_part(stream, dx, dz, (0, 1))
            to_y = 1 - 2 * ((sx + sz // 2) % 2)
            push(t_y(j, odd), t_y(j, odd), ssem.at[3], rty.at[j], at_y(y + to_y, c))
            return
        parity = 0 if stream < 2 else 1 - tree
        await_part(stream, dx, dz, (parity,))
        step = 1 if way[1] == "+" else -1
        to = at(x + step, z) if way[0] == "x" else at(x, z + step)
        applies = (dx + dz + outside) % 2 == parity
        side = (sz if tree == 0 else sx) // 2 % 2
        if way[0] == "z" and abs(dz) == 3:
            applies &= side == (0 if dz > 0 else 1)
        elif way[0] == "x" and abs(dx) == 1:
            applies &= side == (0 if dx > 0 else 1)
        sent[stream] += applies.astype(jnp.int32)

        @pl.when(applies)
        def _():
            push(view(j), view(j), ssem.at[stream], sems.at[j], to)

    def multiply(q, side):
        members = [[offsets[GROUP * q + i] for offsets in BY_PARITY] for i in range(GROUP)]
        for pair in members:
            for o in pair:
                for stream in range(2):
                    await_part(stream, *o, (0,))
        js = [jnp.where(outside == 0, source(*even)[2], source(*odds)[2]) // 2 for even, odds in members]
        rows = slice(256 * side, 256 * (side + 1))
        for g in range(GR):
            left = jnp.concatenate([grads[g, rows, pl.ds(pl.multiple_of(j * HALF, HALF), HALF)] for j in js], axis=1)
            right = jnp.concatenate([big[j, g * HALF : (g + 1) * HALF, :] for j in js], axis=0)
            acc[g, side] += jnp.dot(left, right, preferred_element_type=jnp.float32)

    def targets_done(q):
        squares = tacc[...]
        for dx, dz in OFFSETS[8 * q : 8 * (q + 1)]:
            j = source(dx, dz)[2]
            await_part(2, dx, dz, (0, 1))
            if (dx, dz) != (0, 0):
                await_bytes(t_y(j, 1 - odd), rty.at[j])
            push(tgt.at[j], tgt_in.at[j], ssem.at[8], msem.at[4], sib)
            t = tgt[j].astype(jnp.float32)
            squares += t * t
        tacc[...] = squares

    def share(side):
        total = jnp.zeros((2 * KR * E, KC), jnp.float32)
        for g in range(GR):
            inner = acc[g, side]
            high = inner.astype(jnp.bfloat16)
            low = (inner - high.astype(jnp.float32)).astype(jnp.bfloat16)
            total += jnp.dot(spread[g], high, preferred_element_type=jnp.float32)
            total += jnp.dot(spread[g], low, preferred_element_type=jnp.float32)
        part[side] = total.reshape(2, KR * E, KC)

    def exchange():
        share(1)
        for h in range(2):
            push(part.at[1, h], part_in.at[1 + c], ssem.at[7], csem.at[4 + c], at_y(partner_y(c), h))
        share(0)
        push(part.at[0, 1 - c], part_in.at[0], ssem.at[7], msem.at[3], sib)

    prepared = False
    for kind, i, dx, dz, way in SCHEDULE:
        if kind >= 12 and not prepared:
            prepare()
            prepared = True
        if kind == 12 and i == 0:
            share_candidates()
            await_bytes(cot.at[c], lsem.at[4])
            candidate_grads(c)
        elif kind == 12 and i == 1:
            await_bytes(masked.at[1 - c], msem.at[7])
            await_bytes(cot.at[1 - c], csem.at[0])
            candidate_grads(1 - c)
        elif kind == 12:
            for h in range(2):
                await_bytes(masked.at[2 + h], msem.at[1 + h])
                await_bytes(cot.at[2 + h], csem.at[2 + h])
                candidate_grads(2 + h)
        elif kind == 13:
            multiply(i, 0)
        elif kind == 14:
            multiply(i, 1)
        elif kind == 15:
            targets_done(i)
        elif kind == 16:
            exchange()
        else:
            send(kind, i, dx, dz, way)

    tsq[...] = lax.dot_general(
        jnp.ones((2 * E, KC), jnp.float32), tacc[...], (((1,), (1,)), ((), ())),
        precision=lax.Precision.HIGHEST, preferred_element_type=jnp.float32,
    )
    push(tsq, tsq_in, ssem.at[10], msem.at[6], sib)
    await_bytes(tgt_in, msem.at[4])
    await_bytes(tsq_in, msem.at[6])
    await_bytes(part_in.at[0], msem.at[3])
    for h in range(2):
        await_bytes(part_in.at[1 + h], csem.at[4 + h])

    dots = [[jnp.zeros((4 * E, HALF), jnp.float32) for _ in range(2)] for _ in range(2)]
    squares = jnp.zeros((2 * E, KC), jnp.float32)
    for m in range(KR // 2):
        rows = slice(2 * E * m, 2 * E * (m + 1))
        feat = (part[0, c, rows] + part_in[0, rows]) + (part_in[1, rows] + part_in[2, rows])
        squares += feat * feat
        high = feat.astype(jnp.bfloat16).astype(jnp.float32)
        both = jnp.concatenate([high, feat - high], axis=0).astype(jnp.bfloat16)
        for k in range(2):
            for h, t in enumerate((tgt[2 * m + k], tgt_in[2 * m + k])):
                dots[h][k] += lax.dot_general(both, t, (((1,), (1,)), ((), ())), preferred_element_type=jnp.float32)
    sums = jnp.sum(squares, axis=1, keepdims=True)
    cand_norm = jnp.sqrt(sums[:E] + sums[E:] + EPS)
    scores = []
    for h, t in enumerate((tsq, tsq_in)):
        even, late = dots[h]
        product = (even[:E] + even[2 * E : 3 * E]) + (late[E : 2 * E] + late[3 * E :])
        scores.append(math.sqrt(KR * KC) * product / (cand_norm * jnp.sqrt(t[:E] + EPS)))
    pay[:E] = jnp.where(c == 0, scores[0], scores[1])
    pay[E:] = jnp.where(c == 0, scores[1], scores[0])
    pltpu.make_async_copy(pay, land.at[p], msem.at[5]).start()

    for dx, dz in OFFSETS[:0:-1]:
        push(pay, land.at[p], ssem.at[9], msem.at[5], at(x + dx, z + dz))
    for stream, ref in enumerate((big.at[:, pl.ds(0, ZX_ROWS)], big.at[:, pl.ds(0, XZ_ROWS)], tgt.at[:, pl.ds(0, T_GO)])):

        @pl.loop(0, sent[stream] // 8)
        def _(i):
            await_bytes(ref.at[pl.ds(0, 8)], ssem.at[stream])

        @pl.loop(0, sent[stream] % 8)
        def _(i):
            await_bytes(ref.at[0], ssem.at[stream])

    rest = pl.ds(0, NP - 1)
    await_bytes(tgt.at[rest, pl.ds(0, T_Y)], ssem.at[3])
    await_bytes(tgt.at[0, pl.ds(0, 16 * (YS - 1))], ssem.at[4])

    @pl.when(keeper != c)
    def _():
        await_bytes(tgt.at[0, pl.ds(0, 16)], ssem.at[4])

    await_bytes(masked.at[pl.ds(0, 3)], ssem.at[5])
    await_bytes(cot.at[pl.ds(0, 3)], ssem.at[6])
    await_bytes(tgt_in, ssem.at[8])


    await_bytes(land, msem.at[5])
    for j in range(NP):
        for h in range(2):
            out[E * j : E * (j + 1), HALF * h : HALF * (h + 1)] = land[j, E * h : E * (h + 1)]

    await_bytes(part_in, ssem.at[7])
    await_bytes(land.at[rest], ssem.at[9])
    await_bytes(tsq, ssem.at[10])


def on_device(cotangents, adapter_activations, lengths, column_factors, row_factors, targets):
    anywhere = pl.BlockSpec(memory_space=pl.ANY)
    vmem = pl.BlockSpec(memory_space=pltpu.VMEM)
    bf16, f32 = jnp.bfloat16, jnp.float32
    dma = pltpu.SemaphoreType.DMA
    return pl.pallas_call(
        kernel,
        out_shape=jax.ShapeDtypeStruct((NP * E, 2 * HALF), f32),
        in_specs=[anywhere, anywhere, pl.BlockSpec(memory_space=pltpu.SMEM), anywhere, vmem, anywhere],
        out_specs=vmem,
        scratch_shapes=[
            pltpu.VMEM((4, E, TOK, NB * HALF), bf16),
            pltpu.VMEM((E, TOK, RANK), bf16),
            pltpu.VMEM((4, E, TOK, RANK), bf16),
            pltpu.VMEM((4, E, RANK, TOK), bf16),
            pltpu.VMEM((GR, 4 * E * RS, NB * HALF), bf16),
            pltpu.VMEM((NB, GR * HALF, KC), bf16),
            pltpu.VMEM((NP, HALF, KC), bf16),
            pltpu.VMEM((NP, HALF, KC), bf16),
            pltpu.VMEM((GR, 2, 2 * E * RS, KC), f32),
            pltpu.VMEM((GR, KR * 2 * E, 2 * E * RS), bf16),
            pltpu.VMEM((2, 2, KR * E, KC), f32),
            pltpu.VMEM((3, KR * E, KC), f32),
            pltpu.VMEM((HALF, KC), f32),
            pltpu.VMEM((2 * E, HALF), f32),
            pltpu.VMEM((2 * E, HALF), f32),
            pltpu.VMEM((2 * E, HALF), f32),
            pltpu.VMEM((NP, 2 * E, HALF), f32),
            dma((6,)),
            dma((11,)),
            dma((8,)),
            dma((6,)),
            dma((NP,)),
            dma((NP,)),
            dma((NP,)),
            dma((NP,)),
        ],
        compiler_params=pltpu.CompilerParams(collective_id=0, has_side_effects=True, vmem_limit_bytes=56 * 2**20),
        cost_estimate=pl.CostEstimate(flops=3 * 10**9, bytes_accessed=6 * 2**20, transcendentals=0),
    )(cotangents, adapter_activations, lengths, column_factors, row_factors, targets)


def solution(mesh):
    placed = (
        P(("dp", "proj"), None, None),
        P(("dp", "proj"), None, None),
        P(("dp", "proj")),
        P(None, "proj", None),
        P(),
        P("dp", "proj"),
    )
    return jax.shard_map(on_device, mesh=mesh, in_specs=placed, out_specs=P("dp", None), check_vma=False)
```

time: 79.5 us -> 74.2 us (0.933)
  Pallas kernels: 77.7 us -> 72.4 us
    pallas_call x1, Pallas kernels: 77.7 us -> 72.4 us  [on_device(): pl.pallas_call(kernel, out_shape=jax.ShapeDtypeStruct((NP * E, 2 * HALF),...]
where the time goes in v3:
time: 74.2 us; the launch traced here: 74 us
  Pallas kernels  72.4 us (98%)
  local copies, waits for them, and re-layouts  1.57 us (2%)
    pallas_call x1, Pallas kernels, on_device(): pl.pallas_call(kernel, out_shape=jax.ShapeDtypeStruct((NP * E, 2 * HALF),...  72.4 us
    unnamed x1, local copies, waits for them, and re-layouts  1.57 us

profile of v3, /device:TPU:1, one launch (start us, length us, event | category | flops | bytes accessed | tf_op | source)
XLA Modules:
  0.0 74.0 jit_solution(8392089889903755806)
XLA Ops:
  0.0 72.4 %shard_map.64 = f32[128,256]{1,0:T(8,128)} custom-call(bf16[4,64,8192]{2,1,0:T(8,128)(2,1)} %cot_hbm.1, bf16[4,64,128]{2,1,0:T(8,128)(2,1)} %act_hbm.1, s32[4]{0:T(128)} %lens.1, bf16[4,256,256]{2,1,0:T(8,128)(2,1)} %cf_hbm.1, bf16[4,32,32]{2,1,0:T(8,128)(2,1)} %rf.1, bf16[16,256]{1,0:T(8,128)(2,1)} %tg_hbm.1), custom_call_target="tpu_custom_call" | custom-call | flops 3000000000 | bytes 6291456 | tf_op jit(solution)/shard_map/pallas_call | solution.py:408
  72.4 1.6 %copy.8 = f32[128,256]{1,0:T(8,128)} copy(f32[128,256]{1,0:T(8,128)} %shard_map.64) | data formatting | bytes 262144

commit v4 on v3

--- a/solution.py
+++ b/solution.py
@@ -27,40 +27,40 @@
 BY_PARITY = [[o for o in OFFSETS if sum(o) % 2 == parity] for parity in range(2)]
 GROUP = 4
 SCHEDULE = [
-    (0, 0, 0, 0, "z-"), (1, 1, 0, 0, "x+"), (0, 0, 0, 0, "z+"), (1, 1, 0, 0, "x-"), (12, 0, 0, 0, ""), (2, 0, 0, 0, "z+"),
-    (2, 0, 0, 0, "x-"), (2, 0, 0, 0, "z-"), (2, 0, 0, 0, "x+"), (2, 1, 0, 0, "x+"), (1, 1, -1, 0, "x-"), (1, 1, -1, 0, "z-"),
-    (1, 1, 0, 0, "z-"), (1, 1, -1, 0, "z+"), (1, 1, 0, 0, "z+"), (1, 1, 1, 0, "x+"), (0, 0, 0, 0, "x-"), (2, 1, 0, 0, "z-"),
-    (2, 1, 0, 0, "z+"), (2, 0, 0, 1, "z+"), (2, 0, 0, -1, "x+"), (2, 0, 0, 1, "x+"), (0, 0, 0, 1, "x+"), (2, 0, 0, -1, "x-"),
-    (0, 0, 0, -1, "z-"), (0, 0, 0, -1, "x-"), (0, 0, 0, -1, "x+"), (0, 0, 0, 0, "x+"), (0, 0, 0, 1, "z+"), (2, 0, 0, -1, "z-"),
-    (2, 0, 0, 2, "z+"), (2, 1, 0, 0, "x-"), (0, 0, 0, 1, "x-"), (2, 1, 0, 1, "z+"), (2, 1, 1, 0, "x+"), (2, 1, 1, 0, "z+"),
-    (2, 1, 1, 0, "z-"), (1, 1, 2, 0, "z-"), (2, 0, 0, -2, "z-"), (2, 0, 0, 1, "x-"), (1, 1, 2, 0, "z+"), (0, 0, 0, 2, "x-"),
-    (0, 0, 0, 2, "z+"), (0, 0, 0, -2, "z-"), (0, 0, 0, 2, "x+"), (2, 1, -1, 0, "z-"), (2, 0, 0, -3, "z-"), (2, 0, 0, 2, "x-"),
-    (2, 0, 0, 2, "x+"), (0, 0, 0, -2, "x-"), (2, 1, -1, 0, "x-"), (2, 0, 0, 3, "x-"), (2, 0, 1, 1, "x+"), (2, 0, 0, 3, "x+"),
-    (0, 0, 0, -2, "x+"), (2, 1, -1, 0, "z+"), (2, 0, 0, -2, "x+"), (1, 1, 0, -1, "z-"), (2, 1, 1, -1, "z-"), (1, 1, 1, 0, "z-"),
-    (2, 0, -1, -1, "x-"), (2, 0, 0, -3, "x-"), (2, 0, 0, -2, "x-"), (1, 1, 0, 1, "z+"), (0, 0, 1, 0, "x+"), (2, 0, 1, -1, "x+"),
-    (1, 1, -1, 1, "z+"), (2, 1, -1, -1, "z-"), (2, 0, -1, 2, "x-"), (2, 0, 1, 2, "x+"), (1, 1, -1, -1, "z-"), (1, 1, 1, 0, "z+"),
-    (2, 0, 0, 3, "z+"), (2, 0, -1, 1, "x-"), (1, 1, 2, 1, "z+"), (2, 1, -1, 1, "z+"), (2, 1, 2, 0, "z-"), (2, 0, 0, -3, "x+"),
-    (2, 1, 2, 0, "z+"), (1, 1, 2, -1, "z-"), (0, 0, 0, 3, "z+"), (0, 0, 0, -3, "x-"), (0, 0, 0, -3, "x+"), (0, 0, 1, 1, "x+"),
-    (0, 0, 0, -3, "z-"), (0, 0, 0, 3, "x-"), (0, 0, -1, 0, "x-"), (2, 0, -1, 1, "y"), (12, 1, 0, 0, ""), (1, 1, 1, -1, "z-"),
-    (1, 1, 1, 1, "z+"), (2, 0, -1, -2, "y"), (2, 0, 0, -1, "y"), (0, 0, 1, -1, "x+"), (2, 1, 1, -2, "z-"), (2, 0, 1, -2, "x+"),
-    (0, 0, 0, 3, "x+"), (2, 1, 1, 1, "z+"), (2, 1, 2, 1, "z+"), (2, 1, 0, -1, "z-"), (2, 0, 1, -1, "y"), (2, 0, 0, 4, "x+"),
-    (1, 1, -1, 2, "z+"), (2, 1, -1, -2, "z-"), (0, 0, -1, 1, "x-"), (2, 1, 2, -1, "z-"), (1, 1, 0, 2, "z+"), (0, 0, 1, -2, "x+"),
-    (0, 0, -1, 2, "x-"), (1, 1, 0, -2, "z-"), (2, 0, -1, 2, "y"), (2, 1, 0, 2, "z+"), (2, 1, -1, 2, "z+"), (0, 0, -1, -1, "x-"),
-    (0, 0, 0, 4, "x+"), (0, 0, 0, 4, "x-"), (2, 0, 1, -3, "x+"), (2, 1, 1, -3, "z-"), (2, 0, 2, 1, "y"), (2, 0, 1, 3, "x+"),
-    (2, 0, -1, 0, "x-"), (2, 0, -1, -3, "x-"), (2, 0, -1, 3, "x-"), (1, 1, -1, -2, "z-"), (2, 0, 1, -3, "y"), (1, 1, 1, -2, "z-"),
-    (1, 1, 2, 2, "z+"), (2, 1, 1, 2, "z+"), (2, 1, 0, -2, "z-"), (2, 0, 1, 0, "y"), (2, 0, 1, 0, "x+"), (1, 1, 2, -2, "z-"),
-    (2, 0, 0, 4, "x-"), (1, 1, 1, 2, "z+"), (12, 2, 0, 0, ""), (2, 0, -1, -3, "y"), (2, 0, 2, 2, "y"), (2, 1, 2, -2, "z-"),
-    (2, 1, -1, -3, "z-"), (2, 0, -1, -2, "x-"), (0, 0, -1, 3, "x-"), (2, 0, 2, -1, "y"), (0, 0, 1, -3, "x+"), (2, 1, 1, 3, "z+"),
-    (1, 1, 0, 3, "z+"), (2, 0, -1, 3, "y"), (2, 1, -1, 3, "z+"), (0, 0, 1, 2, "x+"), (0, 0, -1, -2, "x-"), (1, 1, 0, -3, "z-"),
-    (0, 0, 1, 4, "x+"), (0, 0, -1, -3, "x-"), (2, 1, 2, 2, "z+"), (1, 1, -1, -3, "z-"), (1, 1, -1, 3, "z+"), (1, 1, 2, 3, "z+"),
-    (2, 0, 0, 1, "y"), (0, 0, 1, 3, "x+"), (2, 1, 0, 3, "z+"), (2, 1, 0, -3, "z-"), (0, 0, -1, 4, "x-"), (2, 0, 1, 1, "y"),
-    (14, 0, 0, 0, ""), (1, 1, 1, -3, "z-"), (1, 1, 1, 3, "z+"), (13, 1, 0, 0, ""), (2, 0, 0, 2, "y"), (2, 0, 1, -2, "y"),
-    (1, 1, 2, -3, "z-"), (2, 0, 0, 3, "y"), (2, 0, -1, 4, "x-"), (13, 0, 0, 0, ""), (2, 0, -1, -1, "y"), (2, 0, 1, 4, "x+"),
-    (2, 0, 2, -3, "y"), (2, 0, 2, 3, "y"), (14, 1, 0, 0, ""), (2, 1, 2, -3, "z-"), (2, 0, 0, -3, "y"), (2, 0, 0, -2, "y"),
-    (2, 0, 1, 4, "y"), (2, 1, 2, 3, "z+"), (2, 0, -1, 4, "y"), (14, 2, 0, 0, ""), (2, 0, 2, -2, "y"), (2, 0, 1, 3, "y"),
-    (13, 2, 0, 0, ""), (2, 0, 0, 4, "y"), (2, 0, 2, 0, "y"), (2, 0, -1, 0, "y"), (2, 0, 1, 2, "y"), (13, 3, 0, 0, ""),
-    (14, 3, 0, 0, ""), (2, 0, 2, 4, "y"), (16, 0, 0, 0, ""), (15, 2, 0, 0, ""), (15, 3, 0, 0, ""), (15, 0, 0, 0, ""),
-    (15, 1, 0, 0, ""),
+    (0, 0, 0, 0, "z-"), (0, 0, 0, 0, "z+"), (1, 1, 0, 0, "x+"), (1, 1, 0, 0, "x-"), (12, 0, 0, 0, ""), (1, 1, 1, 0, "x+"),
+    (1, 1, -1, 0, "x-"), (0, 0, 0, 0, "x+"), (2, 0, 0, 0, "z-"), (2, 0, 0, 0, "z+"), (0, 0, 0, -1, "z-"), (0, 0, 0, 1, "z+"),
+    (2, 1, 0, 0, "x-"), (0, 0, 0, 1, "x+"), (2, 1, 0, 0, "z-"), (2, 1, 0, 0, "z+"), (1, 1, 0, 0, "z+"), (1, 1, 0, 0, "z-"),
+    (0, 0, 0, -1, "x-"), (2, 0, 0, 0, "x+"), (0, 0, 0, 0, "x-"), (2, 1, 0, 0, "x+"), (1, 1, -1, 0, "z-"), (2, 0, 0, 1, "z+"),
+    (2, 1, -1, 0, "x-"), (1, 1, 1, 0, "z+"), (2, 1, -1, 0, "z-"), (2, 1, 0, 1, "z+"), (2, 0, 0, 1, "x-"), (2, 0, 0, 2, "x+"),
+    (0, 0, 0, 1, "x-"), (2, 0, 0, 2, "z+"), (2, 0, 0, -1, "x+"), (2, 0, 0, -2, "x+"), (2, 0, 0, 2, "x-"), (2, 0, 1, -1, "x+"),
+    (2, 0, 1, 1, "x+"), (2, 1, 0, -1, "z-"), (2, 0, 0, -1, "z-"), (2, 0, 0, -2, "z-"), (1, 1, 2, 0, "z+"), (1, 1, 2, 0, "z-"),
+    (2, 1, 1, 0, "z-"), (2, 0, 0, 1, "x+"), (2, 0, 0, -1, "x-"), (0, 0, 0, -2, "z-"), (0, 0, 0, 2, "z+"), (0, 0, 0, -2, "x+"),
+    (0, 0, 0, 2, "x-"), (1, 1, -1, -1, "z-"), (0, 0, 0, -2, "x-"), (0, 0, 0, 2, "x+"), (1, 1, 1, 1, "z+"), (2, 1, 1, 0, "z+"),
+    (1, 1, 1, 0, "z-"), (2, 1, 1, 0, "x+"), (2, 0, 0, -2, "x-"), (2, 1, -1, 0, "z+"), (2, 0, 0, -3, "z-"), (2, 1, 2, 0, "z-"),
+    (2, 0, -1, 1, "x-"), (1, 1, -1, 0, "z+"), (2, 0, 0, 3, "x+"), (0, 0, 0, -1, "x+"), (2, 0, 0, -3, "x-"), (2, 1, 0, 2, "z+"),
+    (1, 1, 0, -1, "z-"), (2, 1, 2, 0, "z+"), (1, 1, 2, 1, "z+"), (2, 0, 0, 3, "z+"), (2, 0, 0, 1, "y"), (2, 1, -1, -1, "z-"),
+    (2, 0, -1, -1, "x-"), (2, 1, 1, 1, "z+"), (12, 1, 0, 0, ""), (2, 0, 0, 0, "x-"), (2, 0, 0, 3, "x-"), (2, 1, 1, -1, "z-"),
+    (0, 0, 0, -3, "x+"), (2, 0, 1, -2, "x+"), (0, 0, 0, -3, "z-"), (0, 0, 0, 3, "x+"), (0, 0, 0, -3, "x-"), (0, 0, 0, 3, "z+"),
+    (0, 0, 0, 3, "x-"), (2, 0, 0, -3, "x+"), (2, 0, 1, 0, "y"), (1, 1, 0, 1, "z+"), (1, 1, 2, -1, "z-"), (2, 0, 2, -1, "y"),
+    (2, 1, 1, -2, "z-"), (2, 0, 1, -2, "y"), (2, 0, 0, -1, "y"), (2, 0, 1, 3, "x+"), (2, 1, 0, -2, "z-"), (0, 0, -1, 1, "x-"),
+    (2, 1, -1, 1, "z+"), (2, 1, 1, 2, "z+"), (1, 1, -1, 1, "z+"), (2, 0, -1, 0, "y"), (0, 0, -1, -1, "x-"), (2, 1, 2, -1, "z-"),
+    (2, 0, 0, 4, "x+"), (0, 0, 1, 1, "x+"), (2, 0, -1, 2, "x-"), (0, 0, 1, -2, "x+"), (1, 1, 1, -1, "z-"), (2, 0, -1, -2, "y"),
+    (0, 0, -1, -2, "x-"), (0, 0, 1, -1, "x+"), (2, 1, 2, 1, "z+"), (1, 1, 0, -2, "z-"), (2, 0, 1, -1, "y"), (1, 1, 2, 2, "z+"),
+    (2, 0, -1, -1, "y"), (2, 0, -1, -3, "x-"), (2, 0, 1, 2, "x+"), (2, 0, -1, -2, "x-"), (2, 1, -1, 2, "z+"), (0, 0, 0, 4, "x-"),
+    (0, 0, 0, 4, "x+"), (2, 0, 1, 0, "x+"), (0, 0, -1, -3, "x-"), (2, 0, 2, 1, "y"), (1, 1, 2, -2, "z-"), (2, 1, -1, -2, "z-"),
+    (1, 1, 0, 2, "z+"), (2, 1, 1, 3, "z+"), (2, 0, -1, 3, "x-"), (13, 0, 0, 0, ""), (2, 0, 1, 3, "y"), (0, 0, -1, 3, "x-"),
+    (0, 0, 1, 0, "x+"), (2, 0, 0, 3, "y"), (2, 0, 1, -3, "y"), (2, 1, 1, -3, "z-"), (2, 0, 1, -3, "x+"), (1, 1, 1, 2, "z+"),
+    (0, 0, 1, 3, "x+"), (2, 1, 2, 2, "z+"), (0, 0, 1, 2, "x+"), (1, 1, 1, -2, "z-"), (2, 0, -1, 2, "y"), (2, 0, 1, 1, "y"),
+    (2, 1, 2, -2, "z-"), (2, 0, 0, 2, "y"), (2, 0, 0, 4, "x-"), (0, 0, -1, 2, "x-"), (1, 1, -1, -2, "z-"), (0, 0, -1, 0, "x-"),
+    (1, 1, -1, 2, "z+"), (1, 1, 0, -3, "z-"), (1, 1, 2, 3, "z+"), (2, 1, 0, -3, "z-"), (2, 1, -1, -3, "z-"), (0, 0, 1, -3, "x+"),
+    (2, 1, -1, 3, "z+"), (12, 2, 0, 0, ""), (1, 1, 1, 3, "z+"), (2, 0, -1, 0, "x-"), (1, 1, 0, 3, "z+"), (0, 0, 1, 4, "x+"),
+    (2, 0, -1, 3, "y"), (2, 0, -1, 1, "y"), (0, 0, -1, 4, "x-"), (2, 0, -1, 4, "x-"), (2, 1, 2, 3, "z+"), (1, 1, -1, -3, "z-"),
+    (1, 1, 1, -3, "z-"), (2, 0, 1, 2, "y"), (2, 0, 0, -2, "y"), (2, 0, 2, 2, "y"), (1, 1, -1, 3, "z+"), (2, 0, 1, 4, "x+"),
+    (1, 1, 2, -3, "z-"), (13, 1, 0, 0, ""), (2, 0, 0, -3, "y"), (2, 0, 2, -2, "y"), (2, 0, 2, -3, "y"), (2, 1, 0, 3, "z+"),
+    (14, 1, 0, 0, ""), (2, 0, -1, 4, "y"), (2, 1, 2, -3, "z-"), (14, 0, 0, 0, ""), (2, 0, 2, 3, "y"), (2, 0, -1, -3, "y"),
+    (2, 0, 1, 4, "y"), (14, 2, 0, 0, ""), (13, 2, 0, 0, ""), (2, 0, 0, 4, "y"), (2, 0, 2, 0, "y"), (2, 0, 2, 4, "y"),
+    (14, 3, 0, 0, ""), (13, 3, 0, 0, ""), (16, 0, 0, 0, ""), (15, 2, 0, 0, ""), (15, 0, 0, 0, ""), (15, 1, 0, 0, ""),
+    (15, 3, 0, 0, ""),
 ]
 
 
@@ -115,26 +115,18 @@
 
     bar = pltpu.get_barrier_semaphore()
 
-    @pl.loop(1, NP)
-    def _(i):
-        pl.semaphore_signal(bar, inc=1, device_id=(a, (p + i) % NP), device_id_type=MESH)
-
-    @pl.loop(1, 2 * YS)
-    def _(i):
-        pl.semaphore_signal(bar, inc=1, device_id=((a + i) % (2 * YS), p), device_id_type=MESH)
+    greeted = [at(x, z + 1), at(x, z - 1), at(x + 1, z), at(x - 1, z)] + [((a + i) % (2 * YS), p) for i in range(1, 2 * YS)]
+    for to in greeted:
+        pl.semaphore_signal(bar, inc=1, device_id=to, device_id_type=MESH)
 
     own_act.start()
-
-    @pl.loop(0, NB)
-    def _(q):
-        pltpu.make_async_copy(cot_columns(q, odd, c), cot_slot(c, q), lsem.at[4]).start()
 
     @pl.when(outside == 0)
     def _():
         for copy in own:
             copy.wait()
 
-    pl.semaphore_wait(bar, NP - 1 + 2 * YS - 1)
+    pl.semaphore_wait(bar, len(greeted))
 
     keeper = a // YS
     slot = tgt.at[p, pl.ds(pl.multiple_of(16 * (a % YS), 16), 16)]
@@ -170,6 +162,10 @@
         return sx, sz, sx * ZS + sz
 
     def share_candidates():
+        @pl.loop(0, NB)
+        def _(q):
+            pltpu.make_async_copy(cot_columns(q, odd, c), cot_slot(c, q), lsem.at[4]).start()
+
         own_act.wait()
         tokens = lax.broadcasted_iota(jnp.int32, (TOK, RANK), 0)
         for e in range(E):
@@ -275,13 +271,16 @@
             acc[g, side] += jnp.dot(left, right, preferred_element_type=jnp.float32)
 
     def targets_done(q):
-        squares = tacc[...]
+        js = []
         for dx, dz in OFFSETS[8 * q : 8 * (q + 1)]:
             j = source(dx, dz)[2]
             await_part(2, dx, dz, (0, 1))
             if (dx, dz) != (0, 0):
                 await_bytes(t_y(j, 1 - odd), rty.at[j])
             push(tgt.at[j], tgt_in.at[j], ssem.at[8], msem.at[4], sib)
+            js.append(j)
+        squares = tacc[...]
+        for j in js:
             t = tgt[j].astype(jnp.float32)
             squares += t * t
         tacc[...] = squares

time: 74.2 us -> 71.5 us (0.964)
  Pallas kernels: 72.4 us -> 69.7 us
    pallas_call x1, Pallas kernels: 72.4 us -> 69.7 us  [on_device(): pl.pallas_call(kernel, out_shape=jax.ShapeDtypeStruct((NP * E, 2 * HALF),...]
where the time goes in v4:
time: 71.5 us; the launch traced here: 71.2 us
  Pallas kernels  69.7 us (97%)
  local copies, waits for them, and re-layouts  1.57 us (2%)
    pallas_call x1, Pallas kernels, on_device(): pl.pallas_call(kernel, out_shape=jax.ShapeDtypeStruct((NP * E, 2 * HALF),...  69.7 us
    unnamed x1, local copies, waits for them, and re-layouts  1.57 us

profile of v4, /device:TPU:1, one launch (start us, length us, event | category | flops | bytes accessed | tf_op | source)
XLA Modules:
  0.0 71.2 jit_solution(7978260461271991946)
XLA Ops:
  0.0 69.7 %shard_map.64 = f32[128,256]{1,0:T(8,128)} custom-call(bf16[4,64,8192]{2,1,0:T(8,128)(2,1)} %cot_hbm.1, bf16[4,64,128]{2,1,0:T(8,128)(2,1)} %act_hbm.1, s32[4]{0:T(128)} %lens.1, bf16[4,256,256]{2,1,0:T(8,128)(2,1)} %cf_hbm.1, bf16[4,32,32]{2,1,0:T(8,128)(2,1)} %rf.1, bf16[16,256]{1,0:T(8,128)(2,1)} %tg_hbm.1), custom_call_target="tpu_custom_call" | custom-call | flops 3000000000 | bytes 6291456 | tf_op jit(solution)/shard_map/pallas_call | solution.py:407
  69.7 1.6 %copy.8 = f32[128,256]{1,0:T(8,128)} copy(f32[128,256]{1,0:T(8,128)} %shard_map.64) | data formatting | bytes 262144

commit v5 on v4

--- a/solution.py
+++ b/solution.py
@@ -65,8 +65,8 @@
 
 
 def kernel(
-    cot_hbm, act_hbm, lens, cf_hbm, rf, tg_hbm, out,
-    cot, act, masked, flipped, grads, big, tgt, tgt_in, acc, spread, part, part_in, tacc, tsq, tsq_in, pay, land,
+    cot_hbm, act_hbm, lens, cf_hbm, rf, tg_hbm, land,
+    cot, act, masked, flipped, grads, big, tgt, tgt_in, acc, spread, part, part_in, tacc, tsq, tsq_in, pay,
     lsem, ssem, msem, csem, rzx, rxz, rt, rty,
 ):
     a, p = lax.axis_index("dp"), lax.axis_index("proj")
@@ -390,10 +390,6 @@
 
 
     await_bytes(land, msem.at[5])
-    for j in range(NP):
-        for h in range(2):
-            out[E * j : E * (j + 1), HALF * h : HALF * (h + 1)] = land[j, E * h : E * (h + 1)]
-
     await_bytes(part_in, ssem.at[7])
     await_bytes(land.at[rest], ssem.at[9])
     await_bytes(tsq, ssem.at[10])
@@ -404,9 +400,9 @@
     vmem = pl.BlockSpec(memory_space=pltpu.VMEM)
     bf16, f32 = jnp.bfloat16, jnp.float32
     dma = pltpu.SemaphoreType.DMA
-    return pl.pallas_call(
+    scores = pl.pallas_call(
         kernel,
-        out_shape=jax.ShapeDtypeStruct((NP * E, 2 * HALF), f32),
+        out_shape=jax.ShapeDtypeStruct((NP, 2 * E, HALF), f32),
         in_specs=[anywhere, anywhere, pl.BlockSpec(memory_space=pltpu.SMEM), anywhere, vmem, anywhere],
         out_specs=vmem,
         scratch_shapes=[
@@ -426,7 +422,6 @@
             pltpu.VMEM((2 * E, HALF), f32),
             pltpu.VMEM((2 * E, HALF), f32),
             pltpu.VMEM((2 * E, HALF), f32),
-            pltpu.VMEM((NP, 2 * E, HALF), f32),
             dma((6,)),
             dma((11,)),
             dma((8,)),
@@ -439,6 +434,7 @@
         compiler_params=pltpu.CompilerParams(collective_id=0, has_side_effects=True, vmem_limit_bytes=56 * 2**20),
         cost_estimate=pl.CostEstimate(flops=3 * 10**9, bytes_accessed=6 * 2**20, transcendentals=0),
     )(cotangents, adapter_activations, lengths, column_factors, row_factors, targets)
+    return scores.reshape(NP, 2, E, HALF).transpose(0, 2, 1, 3).reshape(NP * E, 2 * HALF)
 
 
 def solution(mesh):

time: 71.5 us -> 71.6 us (level)
    transpose x0 -> x1, local copies, waits for them, and re-layouts: none -> 0.97 us  [on_device(): scores.reshape(NP, 2, E, HALF).transpose(0, 2, 1, 3)]
    unnamed x1, local copies, waits for them, and re-layouts: 1.57 us -> 0.66 us
where the time goes in v5:
time: 71.6 us; the launch traced here: 71.3 us
  Pallas kernels  69.6 us (97%)
  local copies, waits for them, and re-layouts  1.64 us (2%)
    pallas_call x1, Pallas kernels, on_device(): pl.pallas_call(kernel, out_shape=jax.ShapeDtypeStruct((NP, 2 * E, HALF),...  69.6 us

profile of v5, /device:TPU:1, one launch (start us, length us, event | category | flops | bytes accessed | tf_op | source)
XLA Modules:
  0.0 71.3 jit_solution(5337711659698139253)
XLA Ops:
  0.0 69.6 %shard_map.64 = f32[32,8,128]{2,1,0:T(8,128)} custom-call(bf16[4,64,8192]{2,1,0:T(8,128)(2,1)} %cot_hbm.1, bf16[4,64,128]{2,1,0:T(8,128)(2,1)} %act_hbm.1, s32[4]{0:T(128)} %lens.1, bf16[4,256,256]{2,1,0:T(8,128)(2,1)} %cf_hbm.1, bf16[4,32,32]{2,1,0:T(8,128)(2,1)} %rf.1, bf16[16,256]{1,0:T(8,128)(2,1)} %tg_hbm.1), custom_call_target="tpu_custom_call" | custom-call | flops 3000000000 | bytes 6291456 | tf_op jit(solution)/shard_map/pallas_call | solution.py:403
  69.6 1.0 %copy.7 = f32[32,4,2,128]{3,2,1,0:T(2,128)S(1)} copy(f32[32,4,2,128]{3,1,2,0:T(4,128)} %bitcast.9) | data formatting | bytes 262144 | tf_op jit(solution)/shard_map/transpose | solution.py:437
  70.6 0.7 copy.10
